TPU v7x, 256 devices: a whole 4x4x8 slice. The times are simulated.
256 devices in a mesh: clip: 32 (over z, y_lo, core), seq: 8 (over x, y_hi).
Axes of the slice: x: 4, y: 4 (y_hi: 2, y_lo: 2; y = y_hi * 2 + y_lo), z: 8, core: 2. Of those that a mesh axis runs over, the one named last changes fastest.
Arguments:
- query_rows: bfloat16 [32, 1536, 5120], P('clip', 'seq'), may hold values from -32 to 32
- key_rows: bfloat16 [32, 1536, 5120], P('clip', 'seq'), may hold values from -32 to 32
- value_rows: bfloat16 [32, 1536, 5120], P('clip', 'seq'), may hold values from -6 to 6
- query_gain: float32 [5120], replicated, may hold values from 0.1 to 1.9
- key_gain: float32 [5120], replicated, may hold values from 0.1 to 1.9
- tile_lists: int32 [32, 40, 12, 12], P(None, 'seq'), may hold values from 0 to 11, as said below
- tile_counts: int32 [32, 40, 12], P(None, 'seq'), may hold values from 1 to 12, as said below
Outputs:
- attended: bfloat16 [32, 1536, 5120], P('clip', 'seq')
Inputs may be any that keep to these rules, and one draw needn't show every extreme that they name: Each row tile_lists[c, h, b] is a permutation of 0 to 11 whose first entry is b; only its first tile_counts[c, h, b] entries are used. `tile_counts`: some entry equals 12 in every draw.
All inputs are finite; a program needn't handle non-finite values.
Results may differ from a plain program's by a relative error of at most 0.012.
The roundings to bfloat16 on the way count: a program that leaves them out, or rounds other values in their place, can miss the bound.
Values may be sent and summed in bfloat16 or wider, within the bound.
No kernel may reach another device: no remote copies, remote signals or barrier semaphores. Data moves between devices by JAX's collectives and lax.ppermute only.
A program may use at most 128 MiB of HBM per device.

v0:
```python
import math

import jax
import jax.numpy as jnp
from jax import lax
from jax.sharding import PartitionSpec as P

HD = 128
BLK = 128


epsilon = 1e-06


def rms_normed(rows, gain):
    values = rows.astype(jnp.float32)
    spread = jnp.mean(values * values, axis=-1, keepdims=True)
    return (values * lax.rsqrt(spread + epsilon) * gain).astype(jnp.bfloat16)


def attend(query_blocks, key_blocks, value_blocks, lists, counts):
    head_count = query_blocks.shape[2]
    row_blocks = query_blocks.shape[0]
    head_ids = jnp.arange(head_count, dtype=jnp.int32)[:, None]
    last_slot = jnp.max(counts)
    score_scale = 1.0 / math.sqrt(HD)
    initial = (
        jnp.full((head_count, row_blocks, BLK), -1e30, jnp.float32),
        jnp.zeros((head_count, row_blocks, BLK), jnp.float32),
        jnp.zeros((head_count, row_blocks, BLK, HD), jnp.float32),
    )

    def visit_tile(position, carry):
        running_max, running_sum, gathered_sum = carry
        chosen = lax.dynamic_index_in_dim(lists, position, 2, keepdims=False)
        key_tiles = key_blocks[chosen, :, head_ids, :]
        value_tiles = value_blocks[chosen, :, head_ids, :]
        scores = (
            jnp.einsum(
                "rqhd,hrkd->hrqk", query_blocks, key_tiles, preferred_element_type=jnp.float32
            )
            * score_scale
        )
        live_tile = (position < counts)[:, :, None, None]
        scores = jnp.where(live_tile, scores, -1e30)
        new_max = jnp.maximum(running_max, jnp.max(scores, axis=-1))
        decay_factor = jnp.exp(running_max - new_max)
        weights = jnp.exp(scores - new_max[..., None])
        running_sum = running_sum * decay_factor + jnp.sum(weights, axis=-1)
        gathered_sum = gathered_sum * decay_factor[..., None] + jnp.einsum(
            "hrqk,hrkd->hrqd",
            weights.astype(jnp.bfloat16),
            value_tiles,
            preferred_element_type=jnp.float32,
        )
        return (new_max, running_sum, gathered_sum)

    final_state = lax.fori_loop(0, last_slot, visit_tile, initial)
    result = final_state[2] / final_state[1][..., None]
    return jnp.transpose(result, (1, 2, 0, 3)).astype(jnp.bfloat16)


def shards(query_rows, key_rows, value_rows, query_gain, key_gain, tile_lists, tile_counts):
    query_normed = rms_normed(query_rows, query_gain)
    key_normed = rms_normed(key_rows, key_gain)
    heads_query, heads_key, heads_value = (
        lax.all_to_all(query_normed, "seq", split_axis=2, concat_axis=1, tiled=True),
        lax.all_to_all(key_normed, "seq", split_axis=2, concat_axis=1, tiled=True),
        lax.all_to_all(value_rows, "seq", split_axis=2, concat_axis=1, tiled=True),
    )
    local_heads = tile_lists.shape[1]
    length = heads_query.shape[1]
    block_count = length // BLK

    def as_blocks(matrix):
        return matrix.reshape(block_count, BLK, local_heads, HD)

    query_blocks = as_blocks(heads_query)
    key_blocks = as_blocks(heads_key)
    value_blocks = as_blocks(heads_value)
    clip_index = lax.axis_index("clip")
    own_lists = lax.dynamic_index_in_dim(tile_lists, clip_index, 0, keepdims=False)
    own_counts = lax.dynamic_index_in_dim(tile_counts, clip_index, 0, keepdims=False)
    combined = attend(query_blocks, key_blocks, value_blocks, own_lists, own_counts)
    merged = combined.reshape(1, length, local_heads * HD)
    return lax.all_to_all(merged, "seq", split_axis=1, concat_axis=2, tiled=True)


def solution(mesh):
    in_specs = (
        P("clip", "seq", None),
        P("clip", "seq", None),
        P("clip", "seq", None),
        P(),
        P(),
        P(None, "seq", None, None),
        P(None, "seq", None),
    )
    out_specs = P("clip", "seq", None)
    return jax.shard_map(shards, mesh=mesh, in_specs=in_specs, out_specs=out_specs, check_vma=False)
```

profile of v0, /device:TPU:193, one launch (start us, length us, event | category | flops | bytes accessed | tf_op | source)
XLA Modules:
  0.0 528.3 jit_solution(8606463573375375305)
XLA Ops:
  3.5 8.5 %copy.77 = bf16[1,192,5120]{1,0,2:T(2,128)(2,1)} copy(bf16[1,192,5120]{2,1,0:T(8,128)(2,1)S(1)} %fusion.21) | data formatting | bytes 3932160 | tf_op jit(solution)/shard_map/convert_element_type | solution.py:18
  12.6 29.1 %reduce.4 = bf16[5120,192]{1,0:T(8,128)(2,1)S(1)} reduce(bf16[5120,1,192]{2,1,0:T(2,128)(2,1)} %bitcast.85, bf16[]{:T(256)} %broadcast.146), dimensions={1}, to_apply=%bitcast.52.reduce_sub_computation | reduce | bytes 3932162
  41.6 4.8 reshape.98
  46.5 6.8 %all-to-all-start.1 = ((bf16[8,2,61440]{2,1,0:T(2,128)(2,1)}), bf16[8,2,61440]{2,1,0:T(2,128)(2,1)}, u32[]{:S(2)}, u32[]{:S(2)}) async-start(bf16[8,2,61440]{2,1,0:T(2,128)(2,1)} %reshape.98), calls=%async_computation.1 | async-start | bytes 3932160 | tf_op jit(solution)/shard_map/all_to_all | solution.py:67
  55.6 11.3 %copy.74 = bf16[1,192,5120]{1,0,2:T(2,128)(2,1)} copy(bf16[1,192,5120]{2,1,0:T(8,128)(2,1)} %fusion.18) | data formatting | bytes 3932160 | tf_op jit(solution)/shard_map/convert_element_type | solution.py:18
  67.0 29.1 %reduce.3 = bf16[5120,192]{1,0:T(8,128)(2,1)S(1)} reduce(bf16[5120,1,192]{2,1,0:T(2,128)(2,1)} %bitcast.86, bf16[]{:T(256)} %broadcast.146), dimensions={1}, to_apply=%bitcast.50.reduce_sub_computation | reduce | bytes 3932162
  96.0 4.8 reshape.96
  100.8 6.8 %all-to-all-start = ((bf16[8,2,61440]{2,1,0:T(2,128)(2,1)}), bf16[8,2,61440]{2,1,0:T(2,128)(2,1)}, u32[]{:S(2)}, u32[]{:S(2)}) async-start(bf16[8,2,61440]{2,1,0:T(2,128)(2,1)} %reshape.96), calls=%async_computation | async-start | bytes 3932160 | tf_op jit(solution)/shard_map/all_to_all | solution.py:68
  107.6 8.5 %copy.80 = bf16[1,192,5120]{1,0,2:T(2,128)(2,1)} copy(bf16[1,192,5120]{2,1,0:T(8,128)(2,1)S(1)} %copy-done.6) | data formatting | bytes 3932160 | tf_op args[2]
  116.1 29.1 %reduce.5 = bf16[5120,192]{1,0:T(8,128)(2,1)S(1)} reduce(bf16[5120,1,192]{2,1,0:T(2,128)(2,1)} %bitcast.87, bf16[]{:T(256)} %broadcast.146), dimensions={1}, to_apply=%bitcast.54.reduce_sub_computation | reduce | bytes 3932162
  145.2 4.8 reshape.100
  150.0 6.8 %all-to-all-start.2 = ((bf16[8,2,61440]{2,1,0:T(2,128)(2,1)}), bf16[8,2,61440]{2,1,0:T(2,128)(2,1)S(1)}, u32[]{:S(2)}, u32[]{:S(2)}) async-start(bf16[8,2,61440]{2,1,0:T(2,128)(2,1)} %reshape.100), calls=%async_computation.2 | async-start | bytes 3932160 | tf_op jit(solution)/shard_map/all_to_all | solution.py:69
  158.6 7.7 %reshape.99 = bf16[5120,1,192]{2,1,0:T(2,128)(2,1)} reshape(bf16[8,2,61440]{2,1,0:T(2,128)(2,1)} %all-to-all-done.1) | data formatting | bytes 3932160
  166.3 10.9 %copy.78 = bf16[1,192,5120]{2,1,0:T(8,128)(2,1)} copy(bf16[1,192,5120]{1,0,2:T(2,128)(2,1)} %bitcast.82) | data formatting | bytes 3932160 | tf_op jit(solution)/shard_map/all_to_all | solution.py:67
  180.8 5.6 %reshape.72 = bf16[12,128,5,128]{3,2,1,0:T(8,128)(2,1)} reshape(bf16[1,8,192,640]{3,2,1,0:T(8,128)(2,1)} %copy.79) | data formatting | bytes 3932160 | tf_op jit(solution)/shard_map/reshape | solution.py:76
  186.5 3.7 copy.84
  190.2 7.7 %reshape.97 = bf16[5120,1,192]{2,1,0:T(2,128)(2,1)} reshape(bf16[8,2,61440]{2,1,0:T(2,128)(2,1)} %all-to-all-done) | data formatting | bytes 3932160
  197.9 10.9 %copy.75 = bf16[1,192,5120]{2,1,0:T(8,128)(2,1)} copy(bf16[1,192,5120]{1,0,2:T(2,128)(2,1)} %bitcast.83) | data formatting | bytes 3932160 | tf_op jit(solution)/shard_map/all_to_all | solution.py:68
  212.4 5.6 %reshape.71 = bf16[12,128,5,128]{3,2,1,0:T(8,128)(2,1)} reshape(bf16[1,8,192,640]{3,2,1,0:T(8,128)(2,1)} %copy.76) | data formatting | bytes 3932160 | tf_op jit(solution)/shard_map/reshape | solution.py:76
  218.0 3.8 copy.83
  221.8 5.6 %reshape.101 = bf16[5120,1,192]{2,1,0:T(2,128)(2,1)} reshape(bf16[8,2,61440]{2,1,0:T(2,128)(2,1)S(1)} %all-to-all-done.2) | data formatting | bytes 3932160
  227.4 10.0 %copy.81 = bf16[1,192,5120]{2,1,0:T(8,128)(2,1)S(1)} copy(bf16[1,192,5120]{1,0,2:T(2,128)(2,1)} %bitcast.84) | data formatting | bytes 3932160 | tf_op jit(solution)/shard_map/all_to_all | solution.py:69
  241.7 3.8 copy.85
  247.9 214.9 %while.15 = (s32[]{:T(128)}, f32[5,12,128]{2,1,0:T(8,128)S(1)}, f32[5,12,128]{2,1,0:T(8,128)S(1)}, f32[5,12,128,128]{3,2,1,0:T(8,128)}, s32[]{:T(128)}, /*index=...) while((s32[]{:T(128)}, f32[5,12,128]{2,1,0:T(8,128)S(1)}, ...), condition=%wide.region_6.7_spmd.clone, body=%wide.region_3.6_spmd.clone.sunk | while | flops 516111808 | bytes 65374832 | solution.py:58
  251.6 3.8 gather_fusion
  255.4 3.6 bitcast_reduce_fusion.2
  269.4 3.8 gather_fusion
  273.2 3.6 bitcast_reduce_fusion.2
  287.3 3.8 gather_fusion
  291.1 3.6 bitcast_reduce_fusion.2
  305.1 3.8 gather_fusion
  308.9 3.6 bitcast_reduce_fusion.2
  322.9 3.8 gather_fusion
  340.8 3.8 gather_fusion
  344.6 3.6 bitcast_reduce_fusion.2
  358.6 3.8 gather_fusion
  376.4 3.8 gather_fusion
  380.2 3.6 bitcast_reduce_fusion.2
  394.3 3.8 gather_fusion
  412.1 3.8 gather_fusion
  415.9 3.6 bitcast_reduce_fusion.2
  429.9 3.8 gather_fusion
  447.8 3.8 gather_fusion
  451.5 3.6 bitcast_reduce_fusion.2
  468.7 12.8 %reshape.95 = bf16[1,1536,640]{2,0,1:T(2,128)(2,1)} reshape(bf16[12,128,5,128]{3,2,1,0:T(8,128)(2,1)} %copy.90) | data formatting | bytes 3932160 | tf_op jit(solution)/shard_map/reshape | solution.py:85
  481.4 12.2 %reduce.6 = bf16[1536,640]{1,0:T(8,128)(2,1)S(1)} reduce(bf16[1536,1,640]{2,1,0:T(2,128)(2,1)} %bitcast.88, bf16[]{:T(256)} %broadcast.146), dimensions={1}, to_apply=%bitcast.56.reduce_sub_computation | reduce | bytes 3932162
  496.8 23.2 %all_to_all.63 = bf16[8,2,61440]{2,1,0:T(2,128)(2,1)S(1)} all-to-all(bf16[8,2,61440]{2,1,0:T(2,128)(2,1)} %reshape.102), channel_id=1, replica_groups=mesh['clip'=32,'seq'=8] {'seq'}, dimensions={0} | all-to-all | bytes 3932160 | tf_op jit(solution)/shard_map/all_to_all | solution.py:86
  520.0 4.2 reshape.103
  (218 shorter events, 165.2 us)
Async XLA Ops:
  0.0 157.7 %copy-start = (s32[32,5,12,12]{0,3,2,1:T(8,128)S(1)}, s32[32,5,12,12]{0,3,2,1:T(8,128)}, u32[]{:S(2)}) copy-start(s32[32,5,12,12]{0,3,2,1:T(8,128)} %param.14) | copy-start | bytes 276484
  0.0 2.2 copy-start.4
  46.5 6.8 %copy-start.5 = (bf16[1,192,5120]{2,1,0:T(8,128)(2,1)S(1)}, bf16[1,192,5120]{2,1,0:T(8,128)(2,1)}, u32[]{:S(2)}) copy-start(bf16[1,192,5120]{2,1,0:T(8,128)(2,1)} %param.10) | copy-start | bytes 5898244
  46.5 7.3 %copy-start.8 = (f32[5120]{0:T(1024)S(1)}, f32[5120]{0:T(1024)}, u32[]{:S(2)}) copy-start(f32[5120]{0:T(1024)} %param.13) | copy-start | bytes 61444
  46.5 54.3 %all-to-all-start.1 = ((bf16[8,2,61440]{2,1,0:T(2,128)(2,1)}), bf16[8,2,61440]{2,1,0:T(2,128)(2,1)}, u32[]{:S(2)}, u32[]{:S(2)}) async-start(bf16[8,2,61440]{2,1,0:T(2,128)(2,1)} %reshape.98), calls=%async_computation.1 | async-start | bytes 3932160 | tf_op jit(solution)/shard_map/all_to_all | solution.py:67
  100.8 6.8 %copy-start.6 = (bf16[1,192,5120]{2,1,0:T(8,128)(2,1)S(1)}, bf16[1,192,5120]{2,1,0:T(8,128)(2,1)}, u32[]{:S(2)}) copy-start(bf16[1,192,5120]{2,1,0:T(8,128)(2,1)} %param.11) | copy-start | bytes 5898244
  100.8 49.2 %all-to-all-start = ((bf16[8,2,61440]{2,1,0:T(2,128)(2,1)}), bf16[8,2,61440]{2,1,0:T(2,128)(2,1)}, u32[]{:S(2)}, u32[]{:S(2)}) async-start(bf16[8,2,61440]{2,1,0:T(2,128)(2,1)} %reshape.96), calls=%async_computation | async-start | bytes 3932160 | tf_op jit(solution)/shard_map/all_to_all | solution.py:68
  150.0 6.8 %copy-start.7 = (s32[32,5,12]{0,2,1:T(8,128)S(1)}, s32[32,5,12]{0,2,1:T(8,128)}, u32[]{:S(2)}) copy-start(s32[32,5,12]{0,2,1:T(8,128)} %param.15) | copy-start | bytes 23044
  150.0 71.8 %all-to-all-start.2 = ((bf16[8,2,61440]{2,1,0:T(2,128)(2,1)}), bf16[8,2,61440]{2,1,0:T(2,128)(2,1)S(1)}, u32[]{:S(2)}, u32[]{:S(2)}) async-start(bf16[8,2,61440]{2,1,0:T(2,128)(2,1)} %reshape.100), calls=%async_computation.2 | async-start | bytes 3932160 | tf_op jit(solution)/shard_map/all_to_all | solution.py:69
  259.0 2.1 copy-start.2
  264.1 1.9 copy-start.3
  276.9 2.1 copy-start.2
  281.9 1.9 copy-start.3
  294.7 2.1 copy-start.2
  299.7 1.9 copy-start.3
  312.5 2.1 copy-start.2
  317.6 1.9 copy-start.3
  330.4 2.1 copy-start.2
  335.4 1.9 copy-start.3
  348.2 2.1 copy-start.2
  353.2 1.9 copy-start.3
  366.0 2.1 copy-start.2
  371.1 1.9 copy-start.3
  383.9 2.1 copy-start.2
  388.9 1.9 copy-start.3
  401.7 2.1 copy-start.2
  406.7 1.9 copy-start.3
  419.5 2.1 copy-start.2
  424.6 1.9 copy-start.3
  437.4 2.1 copy-start.2
  442.4 1.9 copy-start.3
  455.2 2.1 copy-start.2
  460.2 1.9 copy-start.3
  524.3 4.1 copy-start.1
where the time goes:
time: 532 us; the launch traced here: 528 us
  local copies, waits for them, and re-layouts  275 us (52%)
  other arithmetic  121 us (23%)
  matrix products  78.4 us (15%)
  blocking collectives  23.2 us (4%)
  starting transfers between devices  20.3 us (4%)
  loops' own time  10.1 us (2%)
    unnamed x4, other arithmetic  99.5 us
    unnamed x32, local copies, waits for them, and re-layouts  69.9 us
    gather x12, local copies, waits for them, and re-layouts, visit_tile(): key_tiles = key_blocks[chosen, :, head_ids, :]  45.5 us
    dot_general x12, matrix products, visit_tile(): jnp.einsum('rqhd,hrkd->hrqk', query_blocks, key_tiles, preferred_element_...  43.5 us
    while x60, local copies, waits for them, and re-layouts  36.1 us
    dot_general x12, matrix products, visit_tile(): jnp.einsum('hrqk,hrkd->hrqd', weights.astype(jnp.bfloat16), value_tiles,...  34.9 us
    gather x12, local copies, waits for them, and re-layouts, visit_tile(): value_tiles = value_blocks[chosen, :, head_ids, :]  31.3 us
    all_to_all x1, blocking collectives, shards(): lax.all_to_all(merged, 'seq', split_axis=1, concat_axis=2, tiled=True)  23.2 us
  transfers between devices with their start and end apart: 3, of which 0 were waited for; matrix products, arithmetic and copies ran while one was open for 29% of the time, Pallas kernels for 0%

commit v1 on v0

v1 whole, which is shorter than its diff:
```python
import math

import jax
import jax.numpy as jnp
from jax import lax
from jax.experimental import pallas as pl
from jax.experimental.pallas import tpu as pltpu
from jax.sharding import PartitionSpec as P

HD = 128
BLK = 128
EPSILON = 1e-06
CHUNKS = ((0, 2), (2, 5))
MIB = 1 << 20


def normed(rows, gain):
    values = rows.astype(jnp.float32)
    spread = jnp.mean(values * values, axis=-1, keepdims=True)
    return (values * lax.rsqrt(spread + EPSILON) * gain).astype(jnp.bfloat16)


def pack_heads(query_rows, key_rows, value_rows, query_gain, key_gain, parts, first, last):
    rows, width = query_rows.shape
    own = width // parts
    span = (last - first) * HD
    step = 32

    def kernel(q_ref, k_ref, v_ref, qg_ref, kg_ref, out_ref):
        q = normed(q_ref[...], qg_ref[...])
        k = normed(k_ref[...], kg_ref[...])
        for part in range(parts):
            cols = slice(part * own + first * HD, part * own + last * HD)
            out_ref[part, :, :span] = q[:, cols]
            out_ref[part, :, span : 2 * span] = k[:, cols]
            out_ref[part, :, 2 * span :] = v_ref[:, cols]

    row_spec = pl.BlockSpec((step, width), lambda i: (i, 0))
    gain_spec = pl.BlockSpec((1, width), lambda i: (0, 0))
    return pl.pallas_call(
        kernel,
        grid=(rows // step,),
        in_specs=[row_spec, row_spec, row_spec, gain_spec, gain_spec],
        out_specs=pl.BlockSpec((parts, step, 3 * span), lambda i: (0, i, 0)),
        out_shape=jax.ShapeDtypeStruct((parts, rows, 3 * span), jnp.bfloat16),
        compiler_params=pltpu.CompilerParams(vmem_limit_bytes=56 * MIB),
        cost_estimate=pl.CostEstimate(flops=12 * rows * width, bytes_accessed=12 * rows * width, transcendentals=0),
        name=f"pack_{first}",
    )(query_rows, key_rows, value_rows, query_gain, key_gain)


def attend(packed, bias):
    length = packed.shape[0]
    heads, blocks, _ = bias.shape
    factor = math.log2(math.e) / math.sqrt(HD)

    def kernel(q_ref, k_ref, v_ref, bias_ref, out_ref):
        def block(b, carry):
            rows = pl.ds(pl.multiple_of(b * BLK, BLK), BLK)
            scores = lax.dot_general(
                q_ref[rows, :], k_ref[...], (((1,), (1,)), ((), ())), preferred_element_type=jnp.float32
            )
            scores = scores + bias_ref[0, pl.ds(b, 1), :]
            top = jnp.max(scores, axis=-1, keepdims=True)
            weights = jnp.exp2((scores - top) * factor)
            total = jnp.sum(weights, axis=-1, keepdims=True)
            mixed = jnp.dot(weights.astype(jnp.bfloat16), v_ref[...], preferred_element_type=jnp.float32)
            out_ref[rows, :] = (mixed / total).astype(jnp.bfloat16)
            return carry

        lax.fori_loop(0, blocks, block, 0)

    return pl.pallas_call(
        kernel,
        grid=(heads,),
        in_specs=[
            pl.BlockSpec((length, HD), lambda h: (0, h)),
            pl.BlockSpec((length, HD), lambda h: (0, heads + h)),
            pl.BlockSpec((length, HD), lambda h: (0, 2 * heads + h)),
            pl.BlockSpec((1, blocks, length), lambda h: (h, 0, 0)),
        ],
        out_specs=pl.BlockSpec((length, HD), lambda h: (0, h)),
        out_shape=jax.ShapeDtypeStruct((length, heads * HD), jnp.bfloat16),
        compiler_params=pltpu.CompilerParams(vmem_limit_bytes=56 * MIB),
        cost_estimate=pl.CostEstimate(
            flops=4 * heads * length * length * HD,
            bytes_accessed=8 * heads * length * HD,
            transcendentals=heads * length * length,
        ),
        name=f"attend_{heads}",
    )(packed, packed, packed, bias)


def unpack_heads(pieces):
    parts, rows, _ = pieces[0].shape
    spans = [piece.shape[2] for piece in pieces]
    own = sum(spans)

    def kernel(*refs):
        out_ref = refs[-1]
        at = 0
        for ref, span in zip(refs[:-1], spans):
            out_ref[:, at : at + span] = ref[0]
            at += span

    return pl.pallas_call(
        kernel,
        grid=(parts,),
        in_specs=[pl.BlockSpec((1, rows, span), lambda i: (i, 0, 0)) for span in spans],
        out_specs=pl.BlockSpec((rows, own), lambda i: (0, i)),
        out_shape=jax.ShapeDtypeStruct((rows, parts * own), jnp.bfloat16),
        compiler_params=pltpu.CompilerParams(vmem_limit_bytes=56 * MIB),
        cost_estimate=pl.CostEstimate(flops=0, bytes_accessed=4 * rows * parts * own, transcendentals=0),
        name="unpack",
    )(*pieces)


def swap(blocks):
    return lax.all_to_all(blocks, "seq", 0, 0, tiled=True)


def shards(query_rows, key_rows, value_rows, query_gain, key_gain, tile_lists, tile_counts):
    parts = lax.axis_size("seq")
    _, rows, width = query_rows.shape
    length = rows * parts
    blocks = length // BLK
    heads = tile_lists.shape[1]
    args = (query_rows[0], key_rows[0], value_rows[0], query_gain[None], key_gain[None])
    arrived = []
    for first, last in CHUNKS:
        packed = pack_heads(*args, parts, first, last)
        packed, args, tile_lists, tile_counts = lax.optimization_barrier((packed, args, tile_lists, tile_counts))
        arrived.append(swap(packed))
    clip_index = lax.axis_index("clip")
    lists = lax.dynamic_index_in_dim(tile_lists, clip_index, 0, keepdims=False)
    counts = lax.dynamic_index_in_dim(tile_counts, clip_index, 0, keepdims=False)
    live = jnp.arange(blocks, dtype=jnp.int32) < counts[..., None]
    named = lists[..., None] == (jnp.arange(length, dtype=jnp.int32) // BLK)
    bias = jnp.where(jnp.any(named & live[..., None], axis=2), 0.0, -1e30).astype(jnp.float32)
    sent = []
    for packed, (first, last) in zip(arrived, CHUNKS):
        mixed = attend(packed.reshape(length, packed.shape[2]), bias[first:last])
        sent.append(swap(mixed.reshape(parts, rows, mixed.shape[1])))
    return unpack_heads(sent)[None]


def solution(mesh):
    in_specs = (
        P("clip", "seq", None),
        P("clip", "seq", None),
        P("clip", "seq", None),
        P(),
        P(),
        P(None, "seq", None, None),
        P(None, "seq", None),
    )
    out_specs = P("clip", "seq", None)
    return jax.shard_map(shards, mesh=mesh, in_specs=in_specs, out_specs=out_specs, check_vma=False)
```

time: 532 us -> 165 us (0.31)
  the two profiles are of different devices: /device:TPU:193 before, /device:TPU:2 now
where the time goes in v1:
time: 165 us; the launch traced here: 163 us
  Pallas kernels  60.5 us (37%)
  waiting for transfers between devices  45.9 us (28%)
  blocking collectives  22.7 us (14%)
  starting transfers between devices  21.5 us (13%)
  local copies, waits for them, and re-layouts  10.3 us (6%)
  other arithmetic  1.81 us (1%)
    all_to_all x3, waiting for transfers between devices, swap(): return lax.all_to_all(blocks, 'seq', 0, 0, tiled=True)  45.9 us
    pallas_call x2, Pallas kernels, attend(): pl.pallas_call(kernel, grid=(heads,), in_specs=[pl.BlockSpec((length, HD)...  42.1 us
    all_to_all x1, blocking collectives, swap(): return lax.all_to_all(blocks, 'seq', 0, 0, tiled=True)  22.7 us
    all_to_all x3, starting transfers between devices, swap(): return lax.all_to_all(blocks, 'seq', 0, 0, tiled=True)  21.5 us
    pallas_call x2, Pallas kernels, pack_heads(): pl.pallas_call(kernel, grid=(rows // step,), in_specs=[row_spec, row_spec...  12.7 us
    pallas_call x1, Pallas kernels, unpack_heads(): pl.pallas_call(kernel, grid=(parts,), in_specs=[pl.BlockSpec((1, rows, sp...  5.66 us
    optimization_barrier x2, local copies, waits for them, and re-layouts, shards(): lax.optimization_barrier((packed, args, tile_lists, tile_counts))  4.21 us
  transfers between devices with their start and end apart: 3, of which 2 were waited for; matrix products, arithmetic and copies ran while one was open for 6% of the time, Pallas kernels for 30%

profile of v1, /device:TPU:2, one launch (start us, length us, event | category | flops | bytes accessed | tf_op | source)
XLA Modules:
  0.0 162.6 jit_solution(5672480107663352845)
XLA Ops:
  0.0 6.2 %pack_0.1 = bf16[8,192,768]{2,1,0:T(8,128)(2,1)} custom-call(bf16[192,5120]{1,0:T(8,128)(2,1)} %bitcast.14, bf16[192,5120]{1,0:T(8,128)(2,1)} %bitcast.16, bf16[192,5120]{1,0:T(8,128)(2,1)} %bitcast.18, f32[1,5120]{1,0:T(1,128)} %bitcast.28, f32[1,5120]{1,0:T(1,128)} %bitcast.30), custom_call_target="tpu_custom_call" | custom-call | flops 11796480 | bytes 11796480 | tf_op jit(solution)/shard_map/pack_0/pallas_call | solution.py:40
  6.2 7.5 %all-to-all-start = ((bf16[8,192,768]{2,1,0:T(8,128)(2,1)}), bf16[8,192,768]{2,1,0:T(8,128)(2,1)S(1)}, u32[]{:S(2)}, u32[]{:S(2)}) async-start(bf16[8,192,768]{2,1,0:T(8,128)(2,1)} %pack_0.1), calls=%async_computation | async-start | bytes 4718592 | tf_op jit(solution)/shard_map/all_to_all | solution.py:119
  13.6 6.5 %pack_2.1 = bf16[8,192,1152]{2,1,0:T(8,128)(2,1)} custom-call(bf16[192,5120]{1,0:T(8,128)(2,1)} %bitcast.15, bf16[192,5120]{1,0:T(8,128)(2,1)} %bitcast.17, bf16[192,5120]{1,0:T(8,128)(2,1)} %bitcast.19, f32[1,5120]{1,0:T(1,128)} %bitcast.29, f32[1,5120]{1,0:T(1,128)} %bitcast.31), custom_call_target="tpu_custom_call" | custom-call | flops 11796480 | bytes 11796480 | tf_op jit(solution)/shard_map/pack_2/pallas_call | solution.py:40
  20.2 25.4 %all-to-all-done = bf16[8,192,768]{2,1,0:T(8,128)(2,1)S(1)} async-done(((bf16[8,192,768]{2,1,0:T(8,128)(2,1)}), bf16[8,192,768]{2,1,0:T(8,128)(2,1)S(1)}, u32[]{:S(2)}, u32[]{:S(2)}) %all-to-all-start) | async-done | bytes 2359328 | tf_op jit(solution)/shard_map/all_to_all | solution.py:119
  45.5 0.0 copy-start.1
  45.5 1.4 copy-done.1
  47.0 6.6 %all-to-all-start.2 = ((bf16[8,192,1152]{2,1,0:T(8,128)(2,1)}), bf16[8,192,1152]{2,1,0:T(8,128)(2,1)S(1)}, u32[]{:S(2)}, u32[]{:S(2)}) async-start(bf16[8,192,1152]{2,1,0:T(8,128)(2,1)} %pack_2.1), calls=%async_computation.2 | async-start | bytes 7077888 | tf_op jit(solution)/shard_map/all_to_all | solution.py:119
  53.5 2.7 %copy.11 = s32[32,5,12,12]{3,2,1,0:T(8,128)} copy(s32[32,5,12,12]{0,3,2,1:T(8,128)} %param.12) | data formatting | bytes 184320 | tf_op jit(solution)/shard_map/optimization_barrier | solution.py:132
  56.2 1.6 copy.12
  57.7 0.7 dynamic-slice_bitcast_fusion.1
  58.4 0.8 dynamic-slice_bitcast_fusion
  59.2 0.1 iota_compare_fusion
  59.3 1.7 %and_reduce_fusion = pred[5,12,1536]{2,1,0:T(8,128)(4,1)S(1)} fusion(s32[1536]{0:T(1024)S(1)} %add_select_fusion, s32[5,12,12]{2,1,0:T(8,128)S(1)} %dynamic-slice_bitcast_fusion, pred[5,12,12]{2,1,0:T(8,128)(4,1)S(1)} %iota_compare_fusion), kind=kLoop, calls=%fused_computation | loop fusion | flops 3225600 | bytes 101904 | tf_op jit(solution)/shard_map/reduce_or | solution.py:139
  61.0 0.1 broadcast_select_fusion
  61.0 0.0 copy-start.2
  61.0 0.8 copy-done.2
  61.8 0.7 slice.8.bias_ref
  62.5 17.3 %attend_2.1 = bf16[1536,256]{1,0:T(8,128)(2,1)} custom-call(bf16[1536,768]{1,0:T(8,128)(2,1)} %bitcast.23, bf16[1536,768]{1,0:T(8,128)(2,1)} %bitcast.24, bf16[1536,768]{1,0:T(8,128)(2,1)} %bitcast.25, f32[2,12,1536]{2,1,0:T(8,128)} %slice.8.bias_ref), custom_call_target="tpu_custom_call" | custom-call | flops 2415919104 | bytes 3145728 | tf_op jit(solution)/shard_map/attend_2/pallas_call | solution.py:73
  79.8 20.5 %all-to-all-done.2 = bf16[8,192,1152]{2,1,0:T(8,128)(2,1)S(1)} async-done(((bf16[8,192,1152]{2,1,0:T(8,128)(2,1)}), bf16[8,192,1152]{2,1,0:T(8,128)(2,1)S(1)}, u32[]{:S(2)}, u32[]{:S(2)}) %all-to-all-start.2) | async-done | bytes 3538976 | tf_op jit(solution)/shard_map/all_to_all | solution.py:119
  100.2 0.0 copy-start
  100.2 7.5 %all-to-all-start.1 = ((bf16[8,192,256]{2,1,0:T(8,128)(2,1)}), bf16[8,192,256]{2,1,0:T(8,128)(2,1)}, u32[]{:S(2)}, u32[]{:S(2)}) async-start(bf16[8,192,256]{2,1,0:T(8,128)(2,1)} %bitcast.27), calls=%async_computation.1 | async-start | bytes 1572864 | tf_op jit(solution)/shard_map/all_to_all | solution.py:119
  107.7 1.7 %slice.9.bias_ref = f32[3,12,1536]{2,1,0:T(8,128)} slice(f32[5,12,1536]{2,1,0:T(8,128)} %copy-done.2), slice={[2:5], [0:12], [0:1536]} | slice | bytes 442368 | tf_op jit(solution)/shard_map/slice | solution.py:142
  109.4 0.0 copy-done
  109.4 24.9 %attend_3.1 = bf16[1536,384]{1,0:T(8,128)(2,1)} custom-call(bf16[1536,1152]{1,0:T(8,128)(2,1)} %bitcast.20, bf16[1536,1152]{1,0:T(8,128)(2,1)} %bitcast.21, bf16[1536,1152]{1,0:T(8,128)(2,1)} %bitcast.22, f32[3,12,1536]{2,1,0:T(8,128)} %slice.9.bias_ref), custom_call_target="tpu_custom_call" | custom-call | flops 3623878656 | bytes 4718592 | tf_op jit(solution)/shard_map/attend_3/pallas_call | solution.py:73
  134.3 0.0 all-to-all-done.1.refs_0_
  134.3 22.7 %all_to_all.20.refs_1_ = bf16[8,192,384]{2,1,0:T(8,128)(2,1)} all-to-all(bf16[8,192,384]{2,1,0:T(8,128)(2,1)} %bitcast.26), channel_id=1, replica_groups=mesh['clip'=32,'seq'=8] {'seq'}, dimensions={0} | all-to-all | bytes 2359296 | tf_op jit(solution)/shard_map/all_to_all | solution.py:119
  157.0 5.7 %unpack.1 = bf16[192,5120]{1,0:T(8,128)(2,1)} custom-call(bf16[8,192,256]{2,1,0:T(8,128)(2,1)} %all-to-all-done.1.refs_0_, bf16[8,192,384]{2,1,0:T(8,128)(2,1)} %all_to_all.20.refs_1_), custom_call_target="tpu_custom_call" | custom-call | bytes 3932160 | tf_op jit(solution)/shard_map/unpack/pallas_call | solution.py:106
  (1 shorter events, 0.0 us)
Async XLA Ops:
  6.2 39.4 %all-to-all-start = ((bf16[8,192,768]{2,1,0:T(8,128)(2,1)}), bf16[8,192,768]{2,1,0:T(8,128)(2,1)S(1)}, u32[]{:S(2)}, u32[]{:S(2)}) async-start(bf16[8,192,768]{2,1,0:T(8,128)(2,1)} %pack_0.1), calls=%async_computation | async-start | bytes 4718592 | tf_op jit(solution)/shard_map/all_to_all | solution.py:119
  45.5 1.4 copy-start.1
  47.0 53.3 %all-to-all-start.2 = ((bf16[8,192,1152]{2,1,0:T(8,128)(2,1)}), bf16[8,192,1152]{2,1,0:T(8,128)(2,1)S(1)}, u32[]{:S(2)}, u32[]{:S(2)}) async-start(bf16[8,192,1152]{2,1,0:T(8,128)(2,1)} %pack_2.1), calls=%async_computation.2 | async-start | bytes 7077888 | tf_op jit(solution)/shard_map/all_to_all | solution.py:119
  61.0 0.8 copy-start.2
  100.2 9.2 %copy-start = (bf16[8,192,1152]{2,1,0:T(8,128)(2,1)}, bf16[8,192,1152]{2,1,0:T(8,128)(2,1)S(1)}, u32[]{:S(2)}) copy-start(bf16[8,192,1152]{2,1,0:T(8,128)(2,1)S(1)} %all-to-all-done.2) | copy-start | bytes 10616836
  100.2 34.0 %all-to-all-start.1 = ((bf16[8,192,256]{2,1,0:T(8,128)(2,1)}), bf16[8,192,256]{2,1,0:T(8,128)(2,1)}, u32[]{:S(2)}, u32[]{:S(2)}) async-start(bf16[8,192,256]{2,1,0:T(8,128)(2,1)} %bitcast.27), calls=%async_computation.1 | async-start | bytes 1572864 | tf_op jit(solution)/shard_map/all_to_all | solution.py:119

commit v2 on v1

v2 whole, which is shorter than its diff:
```python
import math

import jax
import jax.numpy as jnp
from jax import lax
from jax.experimental import pallas as pl
from jax.experimental.pallas import tpu as pltpu
from jax.sharding import PartitionSpec as P

HD = 128
BLK = 128
EPSILON = 1e-06
SPLIT = 4
ORDER = ((1, 0), (3, 1), (3, 0), (1, 1), (0, 1), (2, 0), (2, 1))
WINDOW = 5
EARLY = 4
MIB = 1 << 20


def pack_heads(query_rows, key_rows, value_rows, query_gain, key_gain, parts, first, last):
    rows, width = query_rows.shape
    own = width // parts
    span = (last - first) * HD
    step = rows // 2

    def kernel(q_ref, k_ref, v_ref, qg_ref, kg_ref, out_ref):
        def inverse(ref):
            values = ref[...].astype(jnp.float32)
            return lax.rsqrt(jnp.mean(values * values, axis=-1, keepdims=True) + EPSILON)

        def scaled(ref, factor, gain_ref, cols):
            return (ref[:, cols].astype(jnp.float32) * factor * gain_ref[:, cols]).astype(jnp.bfloat16)

        q_factor = inverse(q_ref)
        k_factor = inverse(k_ref)
        for part in range(parts):
            cols = slice(part * own + first * HD, part * own + last * HD)
            out_ref[part, :, :span] = scaled(q_ref, q_factor, qg_ref, cols)
            out_ref[part, :, span : 2 * span] = scaled(k_ref, k_factor, kg_ref, cols)
            out_ref[part, :, 2 * span :] = v_ref[:, cols]

    row_spec = pl.BlockSpec((step, width), lambda i: (i, 0))
    gain_spec = pl.BlockSpec((1, width), lambda i: (0, 0))
    return pl.pallas_call(
        kernel,
        grid=(rows // step,),
        in_specs=[row_spec, row_spec, row_spec, gain_spec, gain_spec],
        out_specs=pl.BlockSpec((parts, step, 3 * span), lambda i: (0, i, 0)),
        out_shape=jax.ShapeDtypeStruct((parts, rows, 3 * span), jnp.bfloat16),
        compiler_params=pltpu.CompilerParams(vmem_limit_bytes=60 * MIB),
        cost_estimate=pl.CostEstimate(flops=12 * rows * width, bytes_accessed=12 * rows * width, transcendentals=0),
        name=f"pack_{first}",
    )(query_rows, key_rows, value_rows, query_gain, key_gain)


def pack_pieces(query_rows, key_rows, value_rows, query_gain, key_gain, targets, first, last):
    rows, width = query_rows.shape
    parts = targets.shape[0]
    own = width // parts
    span = (last - first) * HD
    step = rows // 2

    def kernel(target_ref, q_ref, k_ref, v_ref, qg_ref, kg_ref, *out_refs):
        def inverse(ref):
            values = ref[...].astype(jnp.float32)
            return lax.rsqrt(jnp.mean(values * values, axis=-1, keepdims=True) + EPSILON)

        def scaled(ref, factor, gain_ref, cols):
            return (ref[:, cols].astype(jnp.float32) * factor * gain_ref[:, cols]).astype(jnp.bfloat16)

        q_factor = inverse(q_ref)
        k_factor = inverse(k_ref)
        for o, out_ref in enumerate(out_refs):
            cols = pl.ds(pl.multiple_of(target_ref[o] * own + first * HD, HD), span)
            out_ref[:, :span] = scaled(q_ref, q_factor, qg_ref, cols)
            out_ref[:, span : 2 * span] = scaled(k_ref, k_factor, kg_ref, cols)
            out_ref[:, 2 * span :] = v_ref[:, cols]

    row_spec = pl.BlockSpec((step, width), lambda i, t: (i, 0))
    gain_spec = pl.BlockSpec((1, width), lambda i, t: (0, 0))
    return pl.pallas_call(
        kernel,
        grid_spec=pltpu.PrefetchScalarGridSpec(
            num_scalar_prefetch=1,
            grid=(rows // step,),
            in_specs=[row_spec, row_spec, row_spec, gain_spec, gain_spec],
            out_specs=[pl.BlockSpec((step, 3 * span), lambda i, t: (i, 0))] * parts,
        ),
        out_shape=[jax.ShapeDtypeStruct((rows, 3 * span), jnp.bfloat16)] * parts,
        compiler_params=pltpu.CompilerParams(vmem_limit_bytes=60 * MIB),
        cost_estimate=pl.CostEstimate(flops=12 * rows * width, bytes_accessed=12 * rows * width, transcendentals=0),
        name=f"pack_pieces_{first}",
    )(targets, query_rows, key_rows, value_rows, query_gain, key_gain)


def one_head(q_ref, k_ref, v_ref, bias_ref, out_ref):
    length = q_ref.shape[0]
    factor = math.log2(math.e) / math.sqrt(HD)

    def scored(i):
        raw = lax.dot_general(
            q_ref[i * BLK : (i + 1) * BLK, :],
            k_ref[...],
            (((1,), (1,)), ((), ())),
            preferred_element_type=jnp.float32,
        )
        return raw + bias_ref[i : i + 1, :]

    def finish(i, scores):
        top = jnp.max(scores, axis=-1, keepdims=True)
        weights = jnp.exp2((scores - top) * factor)
        total = jnp.sum(weights, axis=-1, keepdims=True)
        mixed = jnp.dot(weights.astype(jnp.bfloat16), v_ref[...], preferred_element_type=jnp.float32)
        out_ref[i * BLK : (i + 1) * BLK, :] = (mixed / total).astype(jnp.bfloat16)

    scores = scored(0)
    for i in range(length // BLK):
        ahead = scored(i + 1) if (i + 1) * BLK < length else None
        finish(i, scores)
        scores = ahead


def attend_pieces(pieces, bias, sources, first):
    parts = len(pieces)
    rows, width = pieces[0].shape
    heads = width // (3 * HD)
    all_heads, blocks, length = bias.shape

    def kernel(source_ref, bias_ref, *refs):
        in_refs = refs[:parts]
        out_ref, held, done, in_sems, out_sems = refs[parts:]

        def arrival(o, h, j):
            at = pl.multiple_of(source_ref[o] * rows, 64)
            cols = pl.ds((j * heads + h) * HD, HD)
            return pltpu.make_async_copy(in_refs[o].at[:, cols], held.at[pl.ds(at, rows), cols], in_sems.at[h, j, o])

        def departure(h):
            return pltpu.make_async_copy(
                done.at[:, pl.ds(h * HD, HD)], out_ref.at[:, pl.ds((first + h) * HD, HD)], out_sems.at[h]
            )

        for h in range(heads):
            for j in range(3):
                for o in range(parts):
                    arrival(o, h, j).start()
        for h in range(heads):
            for j in range(3):
                for o in range(parts):
                    arrival(o, h, j).wait()
            q, k, v = (held.at[:, (j * heads + h) * HD : (j * heads + h + 1) * HD] for j in range(3))
            one_head(q, k, v, bias_ref.at[first + h], done.at[:, h * HD : (h + 1) * HD])
            departure(h).start()
        for h in range(heads):
            departure(h).wait()

    anywhere = pl.BlockSpec(memory_space=pl.ANY)
    return pl.pallas_call(
        kernel,
        in_specs=[pl.BlockSpec(memory_space=pltpu.SMEM), pl.BlockSpec(memory_space=pltpu.VMEM)]
        + [anywhere] * parts,
        out_specs=anywhere,
        out_shape=jax.ShapeDtypeStruct((length, all_heads * HD), jnp.bfloat16),
        scratch_shapes=[
            pltpu.VMEM((length, width), jnp.bfloat16),
            pltpu.VMEM((length, heads * HD), jnp.bfloat16),
            pltpu.SemaphoreType.DMA((heads, 3, parts)),
            pltpu.SemaphoreType.DMA((heads,)),
        ],
        compiler_params=pltpu.CompilerParams(vmem_limit_bytes=60 * MIB),
        cost_estimate=pl.CostEstimate(
            flops=4 * heads * length * length * HD,
            bytes_accessed=8 * heads * length * HD,
            transcendentals=heads * length * length,
        ),
        name=f"attend_{heads}",
    )(sources, bias, *pieces)


def attend_blocks(packed, bias, first, mixed):
    length, width = packed.shape
    heads = width // (3 * HD)
    blocks = bias.shape[1]

    def kernel(q_ref, k_ref, v_ref, bias_ref, mixed_ref, out_ref):
        one_head(q_ref, k_ref, v_ref, bias_ref.at[0], out_ref)

    return pl.pallas_call(
        kernel,
        grid=(heads,),
        in_specs=[
            pl.BlockSpec((length, HD), lambda h: (0, h)),
            pl.BlockSpec((length, HD), lambda h: (0, heads + h)),
            pl.BlockSpec((length, HD), lambda h: (0, 2 * heads + h)),
            pl.BlockSpec((1, blocks, length), lambda h: (first + h, 0, 0)),
            pl.BlockSpec(memory_space=pl.ANY),
        ],
        out_specs=pl.BlockSpec((length, HD), lambda h: (0, first + h)),
        out_shape=jax.ShapeDtypeStruct(mixed.shape, mixed.dtype),
        input_output_aliases={4: 0},
        compiler_params=pltpu.CompilerParams(vmem_limit_bytes=60 * MIB),
        cost_estimate=pl.CostEstimate(
            flops=4 * heads * length * length * HD,
            bytes_accessed=8 * heads * length * HD,
            transcendentals=heads * length * length,
        ),
        name="attend_blocks",
    )(packed, packed, packed, bias, mixed)


def unpack_heads(pieces):
    parts, rows, _ = pieces[0].shape
    spans = [piece.shape[2] for piece in pieces]
    own = sum(spans)
    step = parts // 2

    def kernel(*refs):
        out_ref = refs[-1]
        at = 0
        for i in range(step):
            for ref, span in zip(refs[:-1], spans):
                out_ref[:, at : at + span] = ref[i]
                at += span

    return pl.pallas_call(
        kernel,
        grid=(parts // step,),
        in_specs=[pl.BlockSpec((step, rows, span), lambda i: (i, 0, 0)) for span in spans],
        out_specs=pl.BlockSpec((rows, step * own), lambda i: (0, i)),
        out_shape=jax.ShapeDtypeStruct((rows, parts * own), jnp.bfloat16),
        compiler_params=pltpu.CompilerParams(vmem_limit_bytes=20 * MIB),
        cost_estimate=pl.CostEstimate(flops=0, bytes_accessed=4 * rows * parts * own, transcendentals=0),
        name="unpack",
    )(*pieces)


def swap(blocks):
    return lax.all_to_all(blocks, "seq", 0, 0, tiled=True)


def ways(parts):
    return [(dx, dy) for dx in range(parts // 2) for dy in range(2)]


def neighbour(index, way, sign, parts):
    x = lax.rem(index // 2 + sign * way[0] + parts // 2, parts // 2)
    y = lax.rem(index % 2 + way[1], 2)
    return 2 * x + y


class Sender:
    def __init__(self, parts):
        self.parts = parts
        self.done = []

    def send(self, piece, way, after=None):
        pairs = []
        for index in range(self.parts):
            x, y = (index // 2 + way[0]) % (self.parts // 2), (index % 2 + way[1]) % 2
            pairs.append((index, 2 * x + y))
        before = self.done[-WINDOW:][:1] if len(self.done) >= WINDOW else []
        if after is not None:
            before = before + [after]
        if before:
            piece, _ = lax.optimization_barrier((piece, before))
        self.done.append(lax.ppermute(piece, "seq", pairs))
        return self.done[-1]

    def send_some(self, pieces, arrived, chosen, after=None):
        all_ways = ways(self.parts)
        for way in chosen:
            arrived[all_ways.index(way)] = self.send(pieces[all_ways.index(way)], way, after)


def shards(query_rows, key_rows, value_rows, query_gain, key_gain, tile_lists, tile_counts):
    parts = lax.axis_size("seq")
    _, rows, width = query_rows.shape
    length = rows * parts
    blocks = length // BLK
    me = lax.axis_index("seq")
    targets = jnp.stack([neighbour(me, way, 1, parts) for way in ways(parts)]).astype(jnp.int32)
    sources = jnp.stack([neighbour(me, way, -1, parts) for way in ways(parts)]).astype(jnp.int32)

    sender = Sender(parts)
    args = (query_rows[0], key_rows[0], value_rows[0], query_gain[None], key_gain[None])
    lead = pack_pieces(*args, targets, 0, SPLIT)
    lead_in = list(lead)
    sender.send_some(lead, lead_in, ORDER)
    args, tile_lists, tile_counts, _ = lax.optimization_barrier((args, tile_lists, tile_counts, sender.done[1]))
    rest = pack_heads(*args, parts, SPLIT, tile_lists.shape[1])
    rest, _ = lax.optimization_barrier((rest, sender.done[EARLY - 1]))
    rest = swap(rest)

    clip_index = lax.axis_index("clip")
    lists = lax.dynamic_index_in_dim(tile_lists, clip_index, 0, keepdims=False)
    counts = lax.dynamic_index_in_dim(tile_counts, clip_index, 0, keepdims=False)
    live = jnp.arange(blocks, dtype=jnp.int32) < counts[..., None]
    named = lists[..., None] == (jnp.arange(length, dtype=jnp.int32) // BLK)
    bias = jnp.where(jnp.any(named & live[..., None], axis=2), 0.0, -1e30).astype(jnp.float32)

    mixed = attend_pieces(lead_in, bias, sources, 0)
    mixed = attend_blocks(rest.reshape(length, rest.shape[2]), bias, SPLIT, mixed)
    home = swap(mixed.reshape(parts, rows, mixed.shape[1]))
    return unpack_heads([home])[None]


def solution(mesh):
    in_specs = (
        P("clip", "seq", None),
        P("clip", "seq", None),
        P("clip", "seq", None),
        P(),
        P(),
        P(None, "seq", None, None),
        P(None, "seq", None),
    )
    out_specs = P("clip", "seq", None)
    return jax.shard_map(shards, mesh=mesh, in_specs=in_specs, out_specs=out_specs, check_vma=False)
```

time: 165 us -> 126 us (0.76); the launches traced: 163 us -> 126 us
  Pallas kernels: 60.5 us -> 34.9 us
  waiting for transfers between devices: 45.9 us -> 27.5 us
  blocking collectives: 22.7 us -> 33 us
  local copies, waits for them, and re-layouts: 10.3 us -> 3.12 us
  starting transfers between devices: 21.5 us -> 24.3 us
    all_to_all x3 -> x1, waiting for transfers between devices: 45.9 us -> 0.01 us  [swap(): return lax.all_to_all(blocks, 'seq', 0, 0, tiled=True)]
    ppermute x0 -> x7, waiting for transfers between devices: none -> 27.5 us  [send(): self.done.append(lax.ppermute(piece, 'seq', pairs))]
    pallas_call x3 -> x4, Pallas kernels: 47.8 us -> 30.9 us  [the longest x1 18.5 us: attend_pieces(): pl.pallas_call(kernel, in_specs=[pl.BlockSpec(memory_space=pltpu.SMEM), p...]
    ppermute x0 -> x7, starting transfers between devices: none -> 16.9 us  [send(): self.done.append(lax.ppermute(piece, 'seq', pairs))]
    all_to_all x3 -> x1, starting transfers between devices: 21.5 us -> 7.4 us  [swap(): return lax.all_to_all(blocks, 'seq', 0, 0, tiled=True)]
    all_to_all x1, blocking collectives: 22.7 us -> 33 us  [swap(): return lax.all_to_all(blocks, 'seq', 0, 0, tiled=True)]
    pallas_call x2 -> x1, Pallas kernels: 12.7 us -> 4.07 us  [pack_heads(): pl.pallas_call(kernel, grid=(rows // step,), in_specs=[row_spec, row_spec...]
    optimization_barrier x2, local copies, waits for them, and re-layouts: 4.21 us -> 0.78 us  [shards(): lax.optimization_barrier((args, tile_lists, tile_counts, sender.done[1]))]
  transfers between devices with their start and end apart: 3 -> 8, of which waited for: 2 -> 6; matrix products, arithmetic and copies ran while one was open for 6% -> 3% of each run, Pallas kernels for 30% -> 18%
where the time goes in v2:
time: 126 us
  Pallas kernels  34.9 us (28%)
  blocking collectives  33 us (26%)
  waiting for transfers between devices  27.5 us (22%)
  starting transfers between devices  24.3 us (19%)
  local copies, waits for them, and re-layouts  3.12 us (2%)
  other arithmetic  2.77 us (2%)
    all_to_all x1, blocking collectives, swap(): return lax.all_to_all(blocks, 'seq', 0, 0, tiled=True)  33 us
    ppermute x7, waiting for transfers between devices, send(): self.done.append(lax.ppermute(piece, 'seq', pairs))  27.5 us
    pallas_call x1, Pallas kernels, attend_pieces(): pl.pallas_call(kernel, in_specs=[pl.BlockSpec(memory_space=pltpu.SMEM), p...  18.5 us
    ppermute x7, starting transfers between devices, send(): self.done.append(lax.ppermute(piece, 'seq', pairs))  16.9 us
    all_to_all x1, starting transfers between devices, swap(): return lax.all_to_all(blocks, 'seq', 0, 0, tiled=True)  7.4 us
    pallas_call x1, Pallas kernels, pack_pieces(): pl.pallas_call(kernel, grid_spec=pltpu.PrefetchScalarGridSpec(num_scalar_...  5.8 us
    pallas_call x1, Pallas kernels, attend_blocks(): pl.pallas_call(kernel, grid=(heads,), in_specs=[pl.BlockSpec((length, HD)...  5.19 us
    pallas_call x1, Pallas kernels, pack_heads(): pl.pallas_call(kernel, grid=(rows // step,), in_specs=[row_spec, row_spec...  4.07 us
  transfers between devices with their start and end apart: 8, of which 6 were waited for; matrix products, arithmetic and copies ran while one was open for 3% of the time, Pallas kernels for 18%

profile of v2, /device:TPU:2, one launch (start us, length us, event | category | flops | bytes accessed | tf_op | source)
XLA Modules:
  0.0 125.7 jit_solution(14810767467146302034)
XLA Ops:
  0.0 0.6 stack.58.target_ref
  0.6 0.0 copy-start.1
  0.6 0.0 copy-start.2
  0.6 5.8 %pack_pieces_0.1 = (bf16[192,1536]{1,0:T(8,128)(2,1)}, bf16[192,1536]{1,0:T(8,128)(2,1)}, bf16[192,1536]{1,0:T(8,128)(2,1)}, bf16[192,1536]{1,0:T(8,128)(2,1)}, ...) custom-call(s32[8]{0:T(128)} %stack.58.target_ref, ...), custom_call_target="tpu_custom_call" | custom-call | flops 11796480 | bytes 11796480 | tf_op jit(solution)/shard_map/pack_pieces_0/pallas_call | solution.py:81
  6.4 1.6 %collective-permute-start.3 = (bf16[192,1536]{1,0:T(8,128)(2,1)}, bf16[192,1536]{1,0:T(8,128)(2,1)S(1)}, u32[]{:S(2)}, u32[]{:S(2)}) collective-permute-start(bf16[192,1536]{1,0:T(8,128)(2,1)} %get-tuple-element.35), channel_id=1, source_target_pairs={{0,2},{1,3},{2,4},{3,5},{4,6},{5,7},{6,0},{7,1},{8,10},{9,11},{10,... | collective-permute-start | bytes 1769480 | tf_op jit(solution)/shard_map/ppermute | solution.py:266
  8.0 3.2 %collective-permute-start = (bf16[192,1536]{1,0:T(8,128)(2,1)}, bf16[192,1536]{1,0:T(8,128)(2,1)S(1)}, u32[]{:S(2)}, u32[]{:S(2)}) collective-permute-start(bf16[192,1536]{1,0:T(8,128)(2,1)} %get-tuple-element.23), channel_id=1, source_target_pairs={{0,7},{1,6},{2,1},{3,0},{4,3},{5,2},{6,5},{7,4},{8,15},{9,14},{10,... | collective-permute-start | bytes 1769480 | tf_op jit(solution)/shard_map/ppermute | solution.py:266
  11.2 1.3 %collective-permute-start.1 = (bf16[192,1536]{1,0:T(8,128)(2,1)}, bf16[192,1536]{1,0:T(8,128)(2,1)}, u32[]{:S(2)}, u32[]{:S(2)}) collective-permute-start(bf16[192,1536]{1,0:T(8,128)(2,1)} %get-tuple-element.29), channel_id=1, source_target_pairs={{0,3},{1,2},{2,5},{3,4},{4,7},{5,6},{6,1},{7,0},{8,11},{9,10},{10,... | collective-permute-start | bytes 1769480 | tf_op jit(solution)/shard_map/ppermute | solution.py:266
  12.4 3.2 %collective-permute-start.2 = (bf16[192,1536]{1,0:T(8,128)(2,1)}, bf16[192,1536]{1,0:T(8,128)(2,1)}, u32[]{:S(2)}, u32[]{:S(2)}) collective-permute-start(bf16[192,1536]{1,0:T(8,128)(2,1)} %get-tuple-element.34), channel_id=1, source_target_pairs={{0,1},{1,0},{2,3},{3,2},{4,5},{5,4},{6,7},{7,6},{8,9},{9,8},{10,11... | collective-permute-start | bytes 1769480 | tf_op jit(solution)/shard_map/ppermute | solution.py:266
  15.6 0.5 collective-permute-start.6
  16.1 0.7 stack.65.source_ref
  16.8 6.4 %collective-permute-done.3.refs_2_ = bf16[192,1536]{1,0:T(8,128)(2,1)S(1)} collective-permute-done((bf16[192,1536]{1,0:T(8,128)(2,1)}, bf16[192,1536]{1,0:T(8,128)(2,1)S(1)}, u32[]{:S(2)}, u32[]{:S(2)}) %collective-permute-start.3) | collective-permute-done | bytes 589856 | tf_op jit(solution)/shard_map/ppermute | solution.py:266
  23.2 0.0 copy-start.3
  23.2 1.8 %collective-permute-start.4 = (bf16[192,1536]{1,0:T(8,128)(2,1)}, bf16[192,1536]{1,0:T(8,128)(2,1)}, u32[]{:S(2)}, u32[]{:S(2)}) collective-permute-start(bf16[192,1536]{1,0:T(8,128)(2,1)} %get-tuple-element.37), channel_id=1, source_target_pairs={{0,4},{1,5},{2,6},{3,7},{4,0},{5,1},{6,2},{7,3},{8,12},{9,13},{10,... | collective-permute-start | bytes 1769480 | tf_op jit(solution)/shard_map/ppermute | solution.py:266
  25.0 3.6 %collective-permute-done.refs_7_ = bf16[192,1536]{1,0:T(8,128)(2,1)S(1)} collective-permute-done((bf16[192,1536]{1,0:T(8,128)(2,1)}, bf16[192,1536]{1,0:T(8,128)(2,1)S(1)}, u32[]{:S(2)}, u32[]{:S(2)}) %collective-permute-start) | collective-permute-done | bytes 589856 | tf_op jit(solution)/shard_map/ppermute | solution.py:266
  28.6 0.0 copy-start.4
  28.6 5.3 %collective-permute-start.5 = (bf16[192,1536]{1,0:T(8,128)(2,1)}, bf16[192,1536]{1,0:T(8,128)(2,1)}, u32[]{:S(2)}, u32[]{:S(2)}) collective-permute-start(bf16[192,1536]{1,0:T(8,128)(2,1)} %get-tuple-element.39), channel_id=1, source_target_pairs={{0,5},{1,4},{2,7},{3,6},{4,1},{5,0},{6,3},{7,2},{8,13},{9,12},{10,... | collective-permute-start | bytes 1769480 | tf_op jit(solution)/shard_map/ppermute | solution.py:266
  33.9 0.0 copy-done.1
  33.9 0.7 copy.12
  34.6 0.0 copy-done.2
  34.6 0.1 copy.13
  34.7 4.1 %pack_4.1 = bf16[8,192,384]{2,1,0:T(8,128)(2,1)} custom-call(bf16[192,5120]{1,0:T(8,128)(2,1)} %bitcast.30, bf16[192,5120]{1,0:T(8,128)(2,1)} %bitcast.32, bf16[192,5120]{1,0:T(8,128)(2,1)} %bitcast.34, f32[1,5120]{1,0:T(1,128)} %bitcast.37, f32[1,5120]{1,0:T(1,128)} %bitcast.39), custom_call_target="tpu_custom_call" | custom-call | flops 11796480 | bytes 11796480 | tf_op jit(solution)/shard_map/pack_4/pallas_call | solution.py:44
  38.8 0.0 copy-done.3
  38.8 0.0 copy-done.4
  38.8 0.1 iota_compare_fusion
  38.9 0.4 collective-permute-done.1.refs_3_
  39.3 7.4 %all-to-all-start = ((bf16[8,192,384]{2,1,0:T(8,128)(2,1)}), bf16[8,192,384]{2,1,0:T(8,128)(2,1)S(1)}, u32[]{:S(2)}, u32[]{:S(2)}) async-start(bf16[8,192,384]{2,1,0:T(8,128)(2,1)} %pack_4.1), calls=%async_computation | async-start | bytes 2359296 | tf_op jit(solution)/shard_map/all_to_all | solution.py:238
  46.7 1.9 %and_reduce_fusion = pred[5,12,1536]{2,1,0:T(8,128)(4,1)S(1)} fusion(s32[1536]{0:T(1024)S(1)} %add_select_fusion, s32[5,12,12]{2,1,0:T(8,128)S(1)} %dynamic-slice_bitcast_fusion, pred[5,12,12]{2,1,0:T(8,128)(4,1)S(1)} %iota_compare_fusion), kind=kLoop, calls=%fused_computation | loop fusion | flops 3225600 | bytes 101904 | tf_op jit(solution)/shard_map/reduce_or | solution.py:299
  48.6 0.8 broadcast_select_fusion.bias_ref
  49.4 2.2 %collective-permute-done.2.refs_1_ = bf16[192,1536]{1,0:T(8,128)(2,1)} collective-permute-done((bf16[192,1536]{1,0:T(8,128)(2,1)}, bf16[192,1536]{1,0:T(8,128)(2,1)}, u32[]{:S(2)}, u32[]{:S(2)}) %collective-permute-start.2) | collective-permute-done | bytes 589856 | tf_op jit(solution)/shard_map/ppermute | solution.py:266
  51.6 0.0 collective-permute-done.6.refs_6_
  51.6 3.4 %collective-permute-done.4.refs_4_ = bf16[192,1536]{1,0:T(8,128)(2,1)} collective-permute-done((bf16[192,1536]{1,0:T(8,128)(2,1)}, bf16[192,1536]{1,0:T(8,128)(2,1)}, u32[]{:S(2)}, u32[]{:S(2)}) %collective-permute-start.4) | collective-permute-done | bytes 589856 | tf_op jit(solution)/shard_map/ppermute | solution.py:266
  55.0 11.5 %collective-permute-done.5.refs_5_ = bf16[192,1536]{1,0:T(8,128)(2,1)} collective-permute-done((bf16[192,1536]{1,0:T(8,128)(2,1)}, bf16[192,1536]{1,0:T(8,128)(2,1)}, u32[]{:S(2)}, u32[]{:S(2)}) %collective-permute-start.5) | collective-permute-done | bytes 589856 | tf_op jit(solution)/shard_map/ppermute | solution.py:266
  66.6 18.5 %attend_4.1.mixed_ref = bf16[1536,640]{1,0:T(8,128)(2,1)} custom-call(s32[8]{0:T(128)} %stack.65.source_ref, f32[5,12,1536]{2,1,0:T(8,128)} %broadcast_select_fusion.bias_ref, bf16[192,1536]{1,0:T(8,128)(2,1)} %get-tuple-element.33.refs_0_, bf16[192,1536]{1,0:T(8,128)(2,1)} %collective-permute-done.2.refs_1_, bf16[192,1536]{1,0:T(8,128)(2,1)} %copy-done.3, ...), custom_call_target="tpu_custom_call" | custom-call | flops 4831838208 | bytes 6291456 | tf_op jit(solution)/shard_map/attend_4/pallas_call | solution.py:158
  85.1 0.0 all-to-all-done
  85.1 0.0 copy-start
  85.1 1.0 copy-done
  86.2 5.2 %attend_blocks.1 = bf16[1536,640]{1,0:T(8,128)(2,1)} custom-call(bf16[1536,384]{1,0:T(8,128)(2,1)} %bitcast.26, bf16[1536,384]{1,0:T(8,128)(2,1)} %bitcast.27, bf16[1536,384]{1,0:T(8,128)(2,1)} %bitcast.28, f32[5,12,1536]{2,1,0:T(8,128)} %broadcast_select_fusion.bias_ref, bf16[1536,640]{1,0:T(8,128)(2,1)} %attend_4.1.mixed_ref), custom_call_target="tpu_custom_call", output_to_operand_aliasing={{}: (4, {})} | custom-call | flops 1207959552 | bytes 1572864 | tf_op jit(solution)/shard_map/attend_blocks/pallas_call | solution.py:188
  91.4 33.0 %all_to_all.10.refs_0_ = bf16[8,192,640]{2,1,0:T(8,128)(2,1)S(1)} all-to-all(bf16[8,192,640]{2,1,0:T(8,128)(2,1)} %bitcast.35), channel_id=1, replica_groups=mesh['clip'=32,'seq'=8] {'seq'}, dimensions={0} | all-to-all | bytes 3932160 | tf_op jit(solution)/shard_map/all_to_all | solution.py:238
  124.4 1.3 %unpack.1 = bf16[192,5120]{1,0:T(8,128)(2,1)} custom-call(bf16[8,192,640]{2,1,0:T(8,128)(2,1)S(1)} %all_to_all.10.refs_0_), custom_call_target="tpu_custom_call" | custom-call | bytes 3932160 | tf_op jit(solution)/shard_map/unpack/pallas_call | solution.py:225
  (3 shorter events, 0.0 us)
Async XLA Ops:
  0.6 33.3 %copy-start.1 = (s32[32,5,12,12]{0,3,2,1:T(8,128)S(1)}, s32[32,5,12,12]{0,3,2,1:T(8,128)}, u32[]{:S(2)}) copy-start(s32[32,5,12,12]{0,3,2,1:T(8,128)} %param.12) | copy-start | bytes 276484
  0.6 34.0 %copy-start.2 = (s32[32,5,12]{0,2,1:T(8,128)S(1)}, s32[32,5,12]{0,2,1:T(8,128)}, u32[]{:S(2)}) copy-start(s32[32,5,12]{0,2,1:T(8,128)} %param.13) | copy-start | bytes 23044
  6.4 16.8 %collective-permute-start.3 = (bf16[192,1536]{1,0:T(8,128)(2,1)}, bf16[192,1536]{1,0:T(8,128)(2,1)S(1)}, u32[]{:S(2)}, u32[]{:S(2)}) collective-permute-start(bf16[192,1536]{1,0:T(8,128)(2,1)} %get-tuple-element.35), channel_id=1, source_target_pairs={{0,2},{1,3},{2,4},{3,5},{4,6},{5,7},{6,0},{7,1},{8,10},{9,11},{10,... | collective-permute-start | bytes 1769480 | tf_op jit(solution)/shard_map/ppermute | solution.py:266
  8.0 20.6 %collective-permute-start = (bf16[192,1536]{1,0:T(8,128)(2,1)}, bf16[192,1536]{1,0:T(8,128)(2,1)S(1)}, u32[]{:S(2)}, u32[]{:S(2)}) collective-permute-start(bf16[192,1536]{1,0:T(8,128)(2,1)} %get-tuple-element.23), channel_id=1, source_target_pairs={{0,7},{1,6},{2,1},{3,0},{4,3},{5,2},{6,5},{7,4},{8,15},{9,14},{10,... | collective-permute-start | bytes 1769480 | tf_op jit(solution)/shard_map/ppermute | solution.py:266
  11.2 28.2 %collective-permute-start.1 = (bf16[192,1536]{1,0:T(8,128)(2,1)}, bf16[192,1536]{1,0:T(8,128)(2,1)}, u32[]{:S(2)}, u32[]{:S(2)}) collective-permute-start(bf16[192,1536]{1,0:T(8,128)(2,1)} %get-tuple-element.29), channel_id=1, source_target_pairs={{0,3},{1,2},{2,5},{3,4},{4,7},{5,6},{6,1},{7,0},{8,11},{9,10},{10,... | collective-permute-start | bytes 1769480 | tf_op jit(solution)/shard_map/ppermute | solution.py:266
  12.4 39.2 %collective-permute-start.2 = (bf16[192,1536]{1,0:T(8,128)(2,1)}, bf16[192,1536]{1,0:T(8,128)(2,1)}, u32[]{:S(2)}, u32[]{:S(2)}) collective-permute-start(bf16[192,1536]{1,0:T(8,128)(2,1)} %get-tuple-element.34), channel_id=1, source_target_pairs={{0,1},{1,0},{2,3},{3,2},{4,5},{5,4},{6,7},{7,6},{8,9},{9,8},{10,11... | collective-permute-start | bytes 1769480 | tf_op jit(solution)/shard_map/ppermute | solution.py:266
  15.6 36.0 %collective-permute-start.6 = (bf16[192,1536]{1,0:T(8,128)(2,1)}, bf16[192,1536]{1,0:T(8,128)(2,1)}, u32[]{:S(2)}, u32[]{:S(2)}) collective-permute-start(bf16[192,1536]{1,0:T(8,128)(2,1)} %get-tuple-element.40), channel_id=1, source_target_pairs={{0,6},{1,7},{2,0},{3,1},{4,2},{5,3},{6,4},{7,5},{8,14},{9,15},{10,... | collective-permute-start | bytes 1769480 | tf_op jit(solution)/shard_map/ppermute | solution.py:266
  23.2 15.6 %copy-start.3 = (bf16[192,1536]{1,0:T(8,128)(2,1)}, bf16[192,1536]{1,0:T(8,128)(2,1)S(1)}, u32[]{:S(2)}) copy-start(bf16[192,1536]{1,0:T(8,128)(2,1)S(1)} %collective-permute-done.3.refs_2_) | copy-start | bytes 1769476
  23.2 31.8 %collective-permute-start.4 = (bf16[192,1536]{1,0:T(8,128)(2,1)}, bf16[192,1536]{1,0:T(8,128)(2,1)}, u32[]{:S(2)}, u32[]{:S(2)}) collective-permute-start(bf16[192,1536]{1,0:T(8,128)(2,1)} %get-tuple-element.37), channel_id=1, source_target_pairs={{0,4},{1,5},{2,6},{3,7},{4,0},{5,1},{6,2},{7,3},{8,12},{9,13},{10,... | collective-permute-start | bytes 1769480 | tf_op jit(solution)/shard_map/ppermute | solution.py:266
  28.6 10.2 %copy-start.4 = (bf16[192,1536]{1,0:T(8,128)(2,1)}, bf16[192,1536]{1,0:T(8,128)(2,1)S(1)}, u32[]{:S(2)}) copy-start(bf16[192,1536]{1,0:T(8,128)(2,1)S(1)} %collective-permute-done.refs_7_) | copy-start | bytes 1769476
  28.6 38.0 %collective-permute-start.5 = (bf16[192,1536]{1,0:T(8,128)(2,1)}, bf16[192,1536]{1,0:T(8,128)(2,1)}, u32[]{:S(2)}, u32[]{:S(2)}) collective-permute-start(bf16[192,1536]{1,0:T(8,128)(2,1)} %get-tuple-element.39), channel_id=1, source_target_pairs={{0,5},{1,4},{2,7},{3,6},{4,1},{5,0},{6,3},{7,2},{8,13},{9,12},{10,... | collective-permute-start | bytes 1769480 | tf_op jit(solution)/shard_map/ppermute | solution.py:266
  39.3 45.8 %all-to-all-start = ((bf16[8,192,384]{2,1,0:T(8,128)(2,1)}), bf16[8,192,384]{2,1,0:T(8,128)(2,1)S(1)}, u32[]{:S(2)}, u32[]{:S(2)}) async-start(bf16[8,192,384]{2,1,0:T(8,128)(2,1)} %pack_4.1), calls=%async_computation | async-start | bytes 2359296 | tf_op jit(solution)/shard_map/all_to_all | solution.py:238
  85.1 1.0 copy-start

commit v3 on v2

--- a/solution.py
+++ b/solution.py
@@ -10,7 +10,7 @@
 HD = 128
 BLK = 128
 EPSILON = 1e-06
-SPLIT = 4
+SPLIT = 3
 ORDER = ((1, 0), (3, 1), (3, 0), (1, 1), (0, 1), (2, 0), (2, 1))
 WINDOW = 5
 EARLY = 4
@@ -169,9 +169,9 @@
         ],
         compiler_params=pltpu.CompilerParams(vmem_limit_bytes=60 * MIB),
         cost_estimate=pl.CostEstimate(
-            flops=4 * heads * length * length * HD,
+            flops=12 * heads * length * length * HD,
             bytes_accessed=8 * heads * length * HD,
-            transcendentals=heads * length * length,
+            transcendentals=3 * heads * length * length,
         ),
         name=f"attend_{heads}",
     )(sources, bias, *pieces)

time: 126 us -> 119 us (0.944)
  waiting for transfers between devices: 27.5 us -> 9.63 us
  starting transfers between devices: 24.3 us -> 39.2 us
  blocking collectives: 33 us -> 28.3 us
  local copies, waits for them, and re-layouts: 3.12 us -> 6 us
  Pallas kernels: 34.9 us -> 33.3 us
    ppermute x7, waiting for transfers between devices: 27.5 us -> 6.44 us  [send(): self.done.append(lax.ppermute(piece, 'seq', pairs))]
    all_to_all x1, starting transfers between devices: 7.4 us -> 22.7 us  [swap(): return lax.all_to_all(blocks, 'seq', 0, 0, tiled=True)]
    pallas_call x1, Pallas kernels: 18.5 us -> 13.7 us  [attend_pieces(): pl.pallas_call(kernel, in_specs=[pl.BlockSpec(memory_space=pltpu.SMEM), p...]
    all_to_all x1, blocking collectives: 33 us -> 28.3 us  [swap(): return lax.all_to_all(blocks, 'seq', 0, 0, tiled=True)]
    pallas_call x1, Pallas kernels: 5.19 us -> 8.52 us  [attend_blocks(): pl.pallas_call(kernel, grid=(heads,), in_specs=[pl.BlockSpec((length, HD)...]
    all_to_all x1, waiting for transfers between devices: 0.01 us -> 3.19 us  [swap(): return lax.all_to_all(blocks, 'seq', 0, 0, tiled=True)]
  transfers between devices with their start and end apart: 8 -> 8, of which waited for: 6 -> 3; matrix products, arithmetic and copies ran while one was open for 3% -> 5% of each run, Pallas kernels for 18% -> 15%
where the time goes in v3:
time: 119 us
  starting transfers between devices  39.2 us (33%)
  Pallas kernels  33.3 us (28%)
  blocking collectives  28.3 us (24%)
  waiting for transfers between devices  9.63 us (8%)
  local copies, waits for them, and re-layouts  6 us (5%)
  other arithmetic  2.61 us (2%)
    all_to_all x1, blocking collectives, swap(): return lax.all_to_all(blocks, 'seq', 0, 0, tiled=True)  28.3 us
    all_to_all x1, starting transfers between devices, swap(): return lax.all_to_all(blocks, 'seq', 0, 0, tiled=True)  22.7 us
    ppermute x7, starting transfers between devices, send(): self.done.append(lax.ppermute(piece, 'seq', pairs))  16.5 us
    pallas_call x1, Pallas kernels, attend_pieces(): pl.pallas_call(kernel, in_specs=[pl.BlockSpec(memory_space=pltpu.SMEM), p...  13.7 us
    pallas_call x1, Pallas kernels, attend_blocks(): pl.pallas_call(kernel, grid=(heads,), in_specs=[pl.BlockSpec((length, HD)...  8.52 us
    ppermute x7, waiting for transfers between devices, send(): self.done.append(lax.ppermute(piece, 'seq', pairs))  6.44 us
    pallas_call x1, Pallas kernels, pack_pieces(): pl.pallas_call(kernel, grid_spec=pltpu.PrefetchScalarGridSpec(num_scalar_...  5.24 us
    pallas_call x1, Pallas kernels, pack_heads(): pl.pallas_call(kernel, grid=(rows // step,), in_specs=[row_spec, row_spec...  4.47 us
  transfers between devices with their start and end apart: 8, of which 3 were waited for; matrix products, arithmetic and copies ran while one was open for 5% of the time, Pallas kernels for 15%

profile of v3, /device:TPU:2, one launch (start us, length us, event | category | flops | bytes accessed | tf_op | source)
XLA Modules:
  0.0 119.1 jit_solution(2841186334213053217)
XLA Ops:
  0.0 0.7 stack.58.target_ref
  0.7 0.0 copy-start.2
  0.7 5.2 %pack_pieces_0.1 = (bf16[192,1152]{1,0:T(8,128)(2,1)}, bf16[192,1152]{1,0:T(8,128)(2,1)}, bf16[192,1152]{1,0:T(8,128)(2,1)}, bf16[192,1152]{1,0:T(8,128)(2,1)}, ...) custom-call(s32[8]{0:T(128)} %stack.58.target_ref, ...), custom_call_target="tpu_custom_call" | custom-call | flops 11796480 | bytes 11796480 | tf_op jit(solution)/shard_map/pack_pieces_0/pallas_call | solution.py:81
  5.9 3.2 %collective-permute-start = (bf16[192,1152]{1,0:T(8,128)(2,1)}, bf16[192,1152]{1,0:T(8,128)(2,1)S(1)}, u32[]{:S(2)}, u32[]{:S(2)}) collective-permute-start(bf16[192,1152]{1,0:T(8,128)(2,1)} %get-tuple-element.23), channel_id=1, source_target_pairs={{0,7},{1,6},{2,1},{3,0},{4,3},{5,2},{6,5},{7,4},{8,15},{9,14},{10,... | collective-permute-start | bytes 1327112 | tf_op jit(solution)/shard_map/ppermute | solution.py:266
  9.2 1.5 %collective-permute-start.3 = (bf16[192,1152]{1,0:T(8,128)(2,1)}, bf16[192,1152]{1,0:T(8,128)(2,1)S(1)}, u32[]{:S(2)}, u32[]{:S(2)}) collective-permute-start(bf16[192,1152]{1,0:T(8,128)(2,1)} %get-tuple-element.35), channel_id=1, source_target_pairs={{0,2},{1,3},{2,4},{3,5},{4,6},{5,7},{6,0},{7,1},{8,10},{9,11},{10,... | collective-permute-start | bytes 1327112 | tf_op jit(solution)/shard_map/ppermute | solution.py:266
  10.7 1.3 %collective-permute-start.1 = (bf16[192,1152]{1,0:T(8,128)(2,1)}, bf16[192,1152]{1,0:T(8,128)(2,1)S(1)}, u32[]{:S(2)}, u32[]{:S(2)}) collective-permute-start(bf16[192,1152]{1,0:T(8,128)(2,1)} %get-tuple-element.29), channel_id=1, source_target_pairs={{0,3},{1,2},{2,5},{3,4},{4,7},{5,6},{6,1},{7,0},{8,11},{9,10},{10,... | collective-permute-start | bytes 1327112 | tf_op jit(solution)/shard_map/ppermute | solution.py:266
  11.9 3.2 %collective-permute-start.2 = (bf16[192,1152]{1,0:T(8,128)(2,1)}, bf16[192,1152]{1,0:T(8,128)(2,1)}, u32[]{:S(2)}, u32[]{:S(2)}) collective-permute-start(bf16[192,1152]{1,0:T(8,128)(2,1)} %get-tuple-element.34), channel_id=1, source_target_pairs={{0,1},{1,0},{2,3},{3,2},{4,5},{5,4},{6,7},{7,6},{8,9},{9,8},{10,11... | collective-permute-start | bytes 1327112 | tf_op jit(solution)/shard_map/ppermute | solution.py:266
  15.1 0.5 collective-permute-start.6
  15.6 0.6 stack.65.source_ref
  16.2 5.5 %collective-permute-done.refs_7_ = bf16[192,1152]{1,0:T(8,128)(2,1)S(1)} collective-permute-done((bf16[192,1152]{1,0:T(8,128)(2,1)}, bf16[192,1152]{1,0:T(8,128)(2,1)S(1)}, u32[]{:S(2)}, u32[]{:S(2)}) %collective-permute-start) | collective-permute-done | bytes 442400 | tf_op jit(solution)/shard_map/ppermute | solution.py:266
  21.7 0.0 copy-start.3
  21.7 0.0 copy-done.2
  21.7 0.1 copy.13
  21.8 6.8 %collective-permute-start.5 = (bf16[192,1152]{1,0:T(8,128)(2,1)}, bf16[192,1152]{1,0:T(8,128)(2,1)}, u32[]{:S(2)}, u32[]{:S(2)}) collective-permute-start(bf16[192,1152]{1,0:T(8,128)(2,1)} %get-tuple-element.39), channel_id=1, source_target_pairs={{0,5},{1,4},{2,7},{3,6},{4,1},{5,0},{6,3},{7,2},{8,13},{9,12},{10,... | collective-permute-start | bytes 1327112 | tf_op jit(solution)/shard_map/ppermute | solution.py:266
  28.6 0.0 collective-permute-done.3.refs_2_
  28.7 0.0 copy-start.4
  28.7 0.0 collective-permute-start.4
  28.7 4.5 %pack_3.1 = bf16[8,192,768]{2,1,0:T(8,128)(2,1)} custom-call(bf16[192,5120]{1,0:T(8,128)(2,1)} %bitcast.30, bf16[192,5120]{1,0:T(8,128)(2,1)} %bitcast.32, bf16[192,5120]{1,0:T(8,128)(2,1)} %bitcast.34, f32[1,5120]{1,0:T(1,128)} %bitcast.37, f32[1,5120]{1,0:T(1,128)} %bitcast.39), custom_call_target="tpu_custom_call" | custom-call | flops 11796480 | bytes 11796480 | tf_op jit(solution)/shard_map/pack_3/pallas_call | solution.py:44
  33.1 0.0 copy-done.3
  33.1 0.0 copy-done.4
  33.1 0.0 copy-start.1
  33.1 0.9 collective-permute-done.1.refs_3_
  34.1 0.0 copy-start.5
  34.1 0.8 copy-done.5
  34.9 22.7 %all-to-all-start = ((bf16[8,192,768]{2,1,0:T(8,128)(2,1)}), bf16[8,192,768]{2,1,0:T(8,128)(2,1)S(1)}, u32[]{:S(2)}, u32[]{:S(2)}) async-start(bf16[8,192,768]{2,1,0:T(8,128)(2,1)} %pack_3.1), calls=%async_computation | async-start | bytes 4718592 | tf_op jit(solution)/shard_map/all_to_all | solution.py:238
  57.6 0.0 copy-done.1
  57.6 1.6 %copy.12 = s32[32,5,12,12]{3,2,1,0:T(8,128)} copy(s32[32,5,12,12]{0,3,2,1:T(8,128)S(1)} %copy-done.1) | data formatting | bytes 184320 | tf_op jit(solution)/shard_map/optimization_barrier | solution.py:289
  59.2 0.8 dynamic-slice_bitcast_fusion
  60.0 0.1 iota_compare_fusion
  60.1 1.7 %and_reduce_fusion = pred[5,12,1536]{2,1,0:T(8,128)(4,1)S(1)} fusion(s32[1536]{0:T(1024)S(1)} %add_select_fusion, s32[5,12,12]{2,1,0:T(8,128)S(1)} %dynamic-slice_bitcast_fusion, pred[5,12,12]{2,1,0:T(8,128)(4,1)S(1)} %iota_compare_fusion), kind=kLoop, calls=%fused_computation | loop fusion | flops 3225600 | bytes 101904 | tf_op jit(solution)/shard_map/reduce_or | solution.py:299
  61.7 0.8 broadcast_select_fusion.bias_ref
  62.6 0.0 collective-permute-done.2.refs_1_
  62.6 0.0 collective-permute-done.6.refs_6_
  62.6 0.0 collective-permute-done.5.refs_5_
  62.6 0.0 collective-permute-done.4.refs_4_
  62.6 13.7 %attend_3.1.mixed_ref = bf16[1536,640]{1,0:T(8,128)(2,1)} custom-call(s32[8]{0:T(128)} %stack.65.source_ref, f32[5,12,1536]{2,1,0:T(8,128)} %broadcast_select_fusion.bias_ref, bf16[192,1152]{1,0:T(8,128)(2,1)} %get-tuple-element.33.refs_0_, bf16[192,1152]{1,0:T(8,128)(2,1)} %collective-permute-done.2.refs_1_, bf16[192,1152]{1,0:T(8,128)(2,1)} %copy-done.4, ...), custom_call_target="tpu_custom_call" | custom-call | flops 10871635968 | bytes 4718592 | tf_op jit(solution)/shard_map/attend_3/pallas_call | solution.py:158
  76.3 3.2 %all-to-all-done = bf16[8,192,768]{2,1,0:T(8,128)(2,1)S(1)} async-done(((bf16[8,192,768]{2,1,0:T(8,128)(2,1)}), bf16[8,192,768]{2,1,0:T(8,128)(2,1)S(1)}, u32[]{:S(2)}, u32[]{:S(2)}) %all-to-all-start) | async-done | bytes 2359328 | tf_op jit(solution)/shard_map/all_to_all | solution.py:238
  79.5 0.0 copy-start
  79.5 1.4 %copy-done = bf16[8,192,768]{2,1,0:T(8,128)(2,1)} copy-done((bf16[8,192,768]{2,1,0:T(8,128)(2,1)}, bf16[8,192,768]{2,1,0:T(8,128)(2,1)S(1)}, u32[]{:S(2)}) %copy-start) | copy-done | bytes 2359320
  80.9 8.5 %attend_blocks.1 = bf16[1536,640]{1,0:T(8,128)(2,1)} custom-call(bf16[1536,768]{1,0:T(8,128)(2,1)} %bitcast.26, bf16[1536,768]{1,0:T(8,128)(2,1)} %bitcast.27, bf16[1536,768]{1,0:T(8,128)(2,1)} %bitcast.28, f32[5,12,1536]{2,1,0:T(8,128)} %broadcast_select_fusion.bias_ref, bf16[1536,640]{1,0:T(8,128)(2,1)} %attend_3.1.mixed_ref), custom_call_target="tpu_custom_call", output_to_operand_aliasing={{}: (4, {})} | custom-call | flops 2415919104 | bytes 3145728 | tf_op jit(solution)/shard_map/attend_blocks/pallas_call | solution.py:188
  89.4 28.3 %all_to_all.10.refs_0_ = bf16[8,192,640]{2,1,0:T(8,128)(2,1)S(1)} all-to-all(bf16[8,192,640]{2,1,0:T(8,128)(2,1)} %bitcast.35), channel_id=1, replica_groups=mesh['clip'=32,'seq'=8] {'seq'}, dimensions={0} | all-to-all | bytes 3932160 | tf_op jit(solution)/shard_map/all_to_all | solution.py:238
  117.7 1.3 %unpack.1 = bf16[192,5120]{1,0:T(8,128)(2,1)} custom-call(bf16[8,192,640]{2,1,0:T(8,128)(2,1)S(1)} %all_to_all.10.refs_0_), custom_call_target="tpu_custom_call" | custom-call | bytes 3932160 | tf_op jit(solution)/shard_map/unpack/pallas_call | solution.py:225
  (2 shorter events, 0.0 us)
Async XLA Ops:
  0.7 21.0 %copy-start.2 = (s32[32,5,12]{0,2,1:T(8,128)S(1)}, s32[32,5,12]{0,2,1:T(8,128)}, u32[]{:S(2)}) copy-start(s32[32,5,12]{0,2,1:T(8,128)} %param.13) | copy-start | bytes 23044
  5.9 15.8 %collective-permute-start = (bf16[192,1152]{1,0:T(8,128)(2,1)}, bf16[192,1152]{1,0:T(8,128)(2,1)S(1)}, u32[]{:S(2)}, u32[]{:S(2)}) collective-permute-start(bf16[192,1152]{1,0:T(8,128)(2,1)} %get-tuple-element.23), channel_id=1, source_target_pairs={{0,7},{1,6},{2,1},{3,0},{4,3},{5,2},{6,5},{7,4},{8,15},{9,14},{10,... | collective-permute-start | bytes 1327112 | tf_op jit(solution)/shard_map/ppermute | solution.py:266
  9.2 19.5 %collective-permute-start.3 = (bf16[192,1152]{1,0:T(8,128)(2,1)}, bf16[192,1152]{1,0:T(8,128)(2,1)S(1)}, u32[]{:S(2)}, u32[]{:S(2)}) collective-permute-start(bf16[192,1152]{1,0:T(8,128)(2,1)} %get-tuple-element.35), channel_id=1, source_target_pairs={{0,2},{1,3},{2,4},{3,5},{4,6},{5,7},{6,0},{7,1},{8,10},{9,11},{10,... | collective-permute-start | bytes 1327112 | tf_op jit(solution)/shard_map/ppermute | solution.py:266
  10.7 23.4 %collective-permute-start.1 = (bf16[192,1152]{1,0:T(8,128)(2,1)}, bf16[192,1152]{1,0:T(8,128)(2,1)S(1)}, u32[]{:S(2)}, u32[]{:S(2)}) collective-permute-start(bf16[192,1152]{1,0:T(8,128)(2,1)} %get-tuple-element.29), channel_id=1, source_target_pairs={{0,3},{1,2},{2,5},{3,4},{4,7},{5,6},{6,1},{7,0},{8,11},{9,10},{10,... | collective-permute-start | bytes 1327112 | tf_op jit(solution)/shard_map/ppermute | solution.py:266
  11.9 50.7 %collective-permute-start.2 = (bf16[192,1152]{1,0:T(8,128)(2,1)}, bf16[192,1152]{1,0:T(8,128)(2,1)}, u32[]{:S(2)}, u32[]{:S(2)}) collective-permute-start(bf16[192,1152]{1,0:T(8,128)(2,1)} %get-tuple-element.34), channel_id=1, source_target_pairs={{0,1},{1,0},{2,3},{3,2},{4,5},{5,4},{6,7},{7,6},{8,9},{9,8},{10,11... | collective-permute-start | bytes 1327112 | tf_op jit(solution)/shard_map/ppermute | solution.py:266
  15.1 47.5 %collective-permute-start.6 = (bf16[192,1152]{1,0:T(8,128)(2,1)}, bf16[192,1152]{1,0:T(8,128)(2,1)}, u32[]{:S(2)}, u32[]{:S(2)}) collective-permute-start(bf16[192,1152]{1,0:T(8,128)(2,1)} %get-tuple-element.40), channel_id=1, source_target_pairs={{0,6},{1,7},{2,0},{3,1},{4,2},{5,3},{6,4},{7,5},{8,14},{9,15},{10,... | collective-permute-start | bytes 1327112 | tf_op jit(solution)/shard_map/ppermute | solution.py:266
  21.7 11.4 %copy-start.3 = (bf16[192,1152]{1,0:T(8,128)(2,1)}, bf16[192,1152]{1,0:T(8,128)(2,1)S(1)}, u32[]{:S(2)}) copy-start(bf16[192,1152]{1,0:T(8,128)(2,1)S(1)} %collective-permute-done.refs_7_) | copy-start | bytes 1327108
  21.8 40.8 %collective-permute-start.5 = (bf16[192,1152]{1,0:T(8,128)(2,1)}, bf16[192,1152]{1,0:T(8,128)(2,1)}, u32[]{:S(2)}, u32[]{:S(2)}) collective-permute-start(bf16[192,1152]{1,0:T(8,128)(2,1)} %get-tuple-element.39), channel_id=1, source_target_pairs={{0,5},{1,4},{2,7},{3,6},{4,1},{5,0},{6,3},{7,2},{8,13},{9,12},{10,... | collective-permute-start | bytes 1327112 | tf_op jit(solution)/shard_map/ppermute | solution.py:266
  28.7 4.5 %copy-start.4 = (bf16[192,1152]{1,0:T(8,128)(2,1)}, bf16[192,1152]{1,0:T(8,128)(2,1)S(1)}, u32[]{:S(2)}) copy-start(bf16[192,1152]{1,0:T(8,128)(2,1)S(1)} %collective-permute-done.3.refs_2_) | copy-start | bytes 1327108
  28.7 33.9 %collective-permute-start.4 = (bf16[192,1152]{1,0:T(8,128)(2,1)}, bf16[192,1152]{1,0:T(8,128)(2,1)}, u32[]{:S(2)}, u32[]{:S(2)}) collective-permute-start(bf16[192,1152]{1,0:T(8,128)(2,1)} %get-tuple-element.37), channel_id=1, source_target_pairs={{0,4},{1,5},{2,6},{3,7},{4,0},{5,1},{6,2},{7,3},{8,12},{9,13},{10,... | collective-permute-start | bytes 1327112 | tf_op jit(solution)/shard_map/ppermute | solution.py:266
  33.1 24.4 %copy-start.1 = (s32[32,5,12,12]{0,3,2,1:T(8,128)S(1)}, s32[32,5,12,12]{0,3,2,1:T(8,128)}, u32[]{:S(2)}) copy-start(s32[32,5,12,12]{0,3,2,1:T(8,128)} %param.12) | copy-start | bytes 276484
  34.1 0.8 copy-start.5
  34.9 44.6 %all-to-all-start = ((bf16[8,192,768]{2,1,0:T(8,128)(2,1)}), bf16[8,192,768]{2,1,0:T(8,128)(2,1)S(1)}, u32[]{:S(2)}, u32[]{:S(2)}) async-start(bf16[8,192,768]{2,1,0:T(8,128)(2,1)} %pack_3.1), calls=%async_computation | async-start | bytes 4718592 | tf_op jit(solution)/shard_map/all_to_all | solution.py:238
  79.5 1.4 %copy-start = (bf16[8,192,768]{2,1,0:T(8,128)(2,1)}, bf16[8,192,768]{2,1,0:T(8,128)(2,1)S(1)}, u32[]{:S(2)}) copy-start(bf16[8,192,768]{2,1,0:T(8,128)(2,1)S(1)} %all-to-all-done) | copy-start | bytes 7077892

commit v4 on v3

--- a/solution.py
+++ b/solution.py
@@ -198,7 +198,7 @@
         out_specs=pl.BlockSpec((length, HD), lambda h: (0, first + h)),
         out_shape=jax.ShapeDtypeStruct(mixed.shape, mixed.dtype),
         input_output_aliases={4: 0},
-        compiler_params=pltpu.CompilerParams(vmem_limit_bytes=60 * MIB),
+        compiler_params=pltpu.CompilerParams(vmem_limit_bytes=28 * MIB),
         cost_estimate=pl.CostEstimate(
             flops=4 * heads * length * length * HD,
             bytes_accessed=8 * heads * length * HD,

time: 119 us -> 118 us (level)
  Pallas kernels: 33.3 us -> 31.8 us
    pallas_call x1, Pallas kernels: 8.52 us -> 7 us  [attend_blocks(): pl.pallas_call(kernel, grid=(heads,), in_specs=[pl.BlockSpec((length, HD)...]
  transfers between devices with their start and end apart: 8 -> 8, of which waited for: 3 -> 3; matrix products, arithmetic and copies ran while one was open for 5% -> 5% of each run, Pallas kernels for 15% -> 16%
where the time goes in v4:
time: 118 us; the launch traced here: 117 us
  starting transfers between devices  39.2 us (33%)
  Pallas kernels  31.8 us (27%)
  blocking collectives  28.1 us (24%)
  waiting for transfers between devices  9.46 us (8%)
  local copies, waits for them, and re-layouts  6.12 us (5%)
  other arithmetic  2.62 us (2%)
    all_to_all x1, blocking collectives, swap(): return lax.all_to_all(blocks, 'seq', 0, 0, tiled=True)  28.1 us
    all_to_all x1, starting transfers between devices, swap(): return lax.all_to_all(blocks, 'seq', 0, 0, tiled=True)  22.7 us
    ppermute x7, starting transfers between devices, send(): self.done.append(lax.ppermute(piece, 'seq', pairs))  16.5 us
    pallas_call x1, Pallas kernels, attend_pieces(): pl.pallas_call(kernel, in_specs=[pl.BlockSpec(memory_space=pltpu.SMEM), p...  13.7 us
    pallas_call x1, Pallas kernels, attend_blocks(): pl.pallas_call(kernel, grid=(heads,), in_specs=[pl.BlockSpec((length, HD)...  7 us
    ppermute x7, waiting for transfers between devices, send(): self.done.append(lax.ppermute(piece, 'seq', pairs))  6.36 us
    pallas_call x1, Pallas kernels, pack_pieces(): pl.pallas_call(kernel, grid_spec=pltpu.PrefetchScalarGridSpec(num_scalar_...  5.23 us
    pallas_call x1, Pallas kernels, pack_heads(): pl.pallas_call(kernel, grid=(rows // step,), in_specs=[row_spec, row_spec...  4.5 us
  transfers between devices with their start and end apart: 8, of which 3 were waited for; matrix products, arithmetic and copies ran while one was open for 5% of the time, Pallas kernels for 16%

profile of v4, /device:TPU:2, one launch (start us, length us, event | category | flops | bytes accessed | tf_op | source)
XLA Modules:
  0.0 117.4 jit_solution(15602922279126155151)
XLA Ops:
  0.0 0.6 stack.58.target_ref
  0.6 0.0 copy-start.3
  0.6 5.2 %pack_pieces_0.1 = (bf16[192,1152]{1,0:T(8,128)(2,1)}, bf16[192,1152]{1,0:T(8,128)(2,1)}, bf16[192,1152]{1,0:T(8,128)(2,1)}, bf16[192,1152]{1,0:T(8,128)(2,1)}, ...) custom-call(s32[8]{0:T(128)} %stack.58.target_ref, ...), custom_call_target="tpu_custom_call" | custom-call | flops 11796480 | bytes 11796480 | tf_op jit(solution)/shard_map/pack_pieces_0/pallas_call | solution.py:81
  5.8 3.2 %collective-permute-start = (bf16[192,1152]{1,0:T(8,128)(2,1)}, bf16[192,1152]{1,0:T(8,128)(2,1)S(1)}, u32[]{:S(2)}, u32[]{:S(2)}) collective-permute-start(bf16[192,1152]{1,0:T(8,128)(2,1)} %get-tuple-element.23), channel_id=1, source_target_pairs={{0,7},{1,6},{2,1},{3,0},{4,3},{5,2},{6,5},{7,4},{8,15},{9,14},{10,... | collective-permute-start | bytes 1327112 | tf_op jit(solution)/shard_map/ppermute | solution.py:266
  9.1 1.5 %collective-permute-start.3 = (bf16[192,1152]{1,0:T(8,128)(2,1)}, bf16[192,1152]{1,0:T(8,128)(2,1)S(1)}, u32[]{:S(2)}, u32[]{:S(2)}) collective-permute-start(bf16[192,1152]{1,0:T(8,128)(2,1)} %get-tuple-element.35), channel_id=1, source_target_pairs={{0,2},{1,3},{2,4},{3,5},{4,6},{5,7},{6,0},{7,1},{8,10},{9,11},{10,... | collective-permute-start | bytes 1327112 | tf_op jit(solution)/shard_map/ppermute | solution.py:266
  10.6 1.3 %collective-permute-start.1 = (bf16[192,1152]{1,0:T(8,128)(2,1)}, bf16[192,1152]{1,0:T(8,128)(2,1)S(1)}, u32[]{:S(2)}, u32[]{:S(2)}) collective-permute-start(bf16[192,1152]{1,0:T(8,128)(2,1)} %get-tuple-element.29), channel_id=1, source_target_pairs={{0,3},{1,2},{2,5},{3,4},{4,7},{5,6},{6,1},{7,0},{8,11},{9,10},{10,... | collective-permute-start | bytes 1327112 | tf_op jit(solution)/shard_map/ppermute | solution.py:266
  11.8 3.2 %collective-permute-start.2 = (bf16[192,1152]{1,0:T(8,128)(2,1)}, bf16[192,1152]{1,0:T(8,128)(2,1)}, u32[]{:S(2)}, u32[]{:S(2)}) collective-permute-start(bf16[192,1152]{1,0:T(8,128)(2,1)} %get-tuple-element.34), channel_id=1, source_target_pairs={{0,1},{1,0},{2,3},{3,2},{4,5},{5,4},{6,7},{7,6},{8,9},{9,8},{10,11... | collective-permute-start | bytes 1327112 | tf_op jit(solution)/shard_map/ppermute | solution.py:266
  15.0 0.5 collective-permute-start.6
  15.6 0.6 stack.65.source_ref
  16.2 5.4 %collective-permute-done.refs_7_ = bf16[192,1152]{1,0:T(8,128)(2,1)S(1)} collective-permute-done((bf16[192,1152]{1,0:T(8,128)(2,1)}, bf16[192,1152]{1,0:T(8,128)(2,1)S(1)}, u32[]{:S(2)}, u32[]{:S(2)}) %collective-permute-start) | collective-permute-done | bytes 442400 | tf_op jit(solution)/shard_map/ppermute | solution.py:266
  21.6 0.0 copy-start.4
  21.6 0.0 copy-done.3
  21.6 0.1 copy.13
  21.8 6.8 %collective-permute-start.5 = (bf16[192,1152]{1,0:T(8,128)(2,1)}, bf16[192,1152]{1,0:T(8,128)(2,1)}, u32[]{:S(2)}, u32[]{:S(2)}) collective-permute-start(bf16[192,1152]{1,0:T(8,128)(2,1)} %get-tuple-element.39), channel_id=1, source_target_pairs={{0,5},{1,4},{2,7},{3,6},{4,1},{5,0},{6,3},{7,2},{8,13},{9,12},{10,... | collective-permute-start | bytes 1327112 | tf_op jit(solution)/shard_map/ppermute | solution.py:266
  28.6 0.0 collective-permute-done.3.refs_2_
  28.6 0.0 copy-start.5
  28.6 0.0 collective-permute-start.4
  28.6 4.5 %pack_3.1 = bf16[8,192,768]{2,1,0:T(8,128)(2,1)} custom-call(bf16[192,5120]{1,0:T(8,128)(2,1)} %bitcast.31, bf16[192,5120]{1,0:T(8,128)(2,1)} %bitcast.33, bf16[192,5120]{1,0:T(8,128)(2,1)} %bitcast.35, f32[1,5120]{1,0:T(1,128)} %bitcast.37, f32[1,5120]{1,0:T(1,128)} %bitcast.39), custom_call_target="tpu_custom_call" | custom-call | flops 11796480 | bytes 11796480 | tf_op jit(solution)/shard_map/pack_3/pallas_call | solution.py:44
  33.1 0.0 copy-done.4
  33.1 0.0 copy-done.5
  33.1 0.0 copy-start.2
  33.1 0.9 collective-permute-done.1.refs_3_
  34.0 0.0 copy-start.6
  34.0 0.8 copy-done.6
  34.8 22.7 %all-to-all-start = ((bf16[8,192,768]{2,1,0:T(8,128)(2,1)}), bf16[8,192,768]{2,1,0:T(8,128)(2,1)S(1)}, u32[]{:S(2)}, u32[]{:S(2)}) async-start(bf16[8,192,768]{2,1,0:T(8,128)(2,1)} %pack_3.1), calls=%async_computation | async-start | bytes 4718592 | tf_op jit(solution)/shard_map/all_to_all | solution.py:238
  57.5 0.0 copy-done.2
  57.5 1.6 %copy.12 = s32[32,5,12,12]{3,2,1,0:T(8,128)} copy(s32[32,5,12,12]{0,3,2,1:T(8,128)S(1)} %copy-done.2) | data formatting | bytes 184320 | tf_op jit(solution)/shard_map/optimization_barrier | solution.py:289
  59.1 0.8 dynamic-slice_bitcast_fusion
  59.9 0.1 iota_compare_fusion
  60.0 1.7 %and_reduce_fusion = pred[5,12,1536]{2,1,0:T(8,128)(4,1)S(1)} fusion(s32[1536]{0:T(1024)S(1)} %add_select_fusion, s32[5,12,12]{2,1,0:T(8,128)S(1)} %dynamic-slice_bitcast_fusion, pred[5,12,12]{2,1,0:T(8,128)(4,1)S(1)} %iota_compare_fusion), kind=kLoop, calls=%fused_computation | loop fusion | flops 3225600 | bytes 101904 | tf_op jit(solution)/shard_map/reduce_or | solution.py:299
  61.7 0.9 broadcast_select_fusion.bias_ref
  62.5 0.0 collective-permute-done.2.refs_1_
  62.5 0.0 collective-permute-done.6.refs_6_
  62.5 0.0 collective-permute-done.5.refs_5_
  62.5 0.0 collective-permute-done.4.refs_4_
  62.6 0.0 copy-start.1
  62.6 13.7 %attend_3.1.mixed_ref = bf16[1536,640]{1,0:T(8,128)(2,1)} custom-call(s32[8]{0:T(128)} %stack.65.source_ref, f32[5,12,1536]{2,1,0:T(8,128)} %broadcast_select_fusion.bias_ref, bf16[192,1152]{1,0:T(8,128)(2,1)} %get-tuple-element.33.refs_0_, bf16[192,1152]{1,0:T(8,128)(2,1)} %collective-permute-done.2.refs_1_, bf16[192,1152]{1,0:T(8,128)(2,1)} %copy-done.5, ...), custom_call_target="tpu_custom_call" | custom-call | flops 10871635968 | bytes 4718592 | tf_op jit(solution)/shard_map/attend_3/pallas_call | solution.py:158
  76.3 3.1 %all-to-all-done = bf16[8,192,768]{2,1,0:T(8,128)(2,1)S(1)} async-done(((bf16[8,192,768]{2,1,0:T(8,128)(2,1)}), bf16[8,192,768]{2,1,0:T(8,128)(2,1)S(1)}, u32[]{:S(2)}, u32[]{:S(2)}) %all-to-all-start) | async-done | bytes 2359328 | tf_op jit(solution)/shard_map/all_to_all | solution.py:238
  79.4 0.0 copy-done.1
  79.4 0.0 copy-start
  79.4 1.5 %copy-done = bf16[1536,640]{1,0:T(8,128)(2,1)S(1)} copy-done((bf16[1536,640]{1,0:T(8,128)(2,1)S(1)}, bf16[1536,640]{1,0:T(8,128)(2,1)}, u32[]{:S(2)}) %copy-start) | copy-done | bytes 1966104
  81.0 7.0 %attend_blocks.1 = bf16[1536,640]{1,0:T(8,128)(2,1)S(1)} custom-call(bf16[1536,768]{1,0:T(8,128)(2,1)S(1)} %bitcast.26, bf16[1536,768]{1,0:T(8,128)(2,1)S(1)} %bitcast.27, bf16[1536,768]{1,0:T(8,128)(2,1)S(1)} %bitcast.28, f32[5,12,1536]{2,1,0:T(8,128)S(1)} %copy-done.1, bf16[1536,640]{1,0:T(8,128)(2,1)S(1)} %copy-done), custom_call_target="tpu_custom_call", output_to_operand_aliasing={{}: (4, {})} | custom-call | flops 2415919104 | bytes 3145728 | tf_op jit(solution)/shard_map/attend_blocks/pallas_call | solution.py:188
  88.0 28.1 %all_to_all.10.refs_0_ = bf16[8,192,640]{2,1,0:T(8,128)(2,1)S(1)} all-to-all(bf16[8,192,640]{2,1,0:T(8,128)(2,1)S(1)} %bitcast.29), channel_id=1, replica_groups=mesh['clip'=32,'seq'=8] {'seq'}, dimensions={0} | all-to-all | bytes 3932160 | tf_op jit(solution)/shard_map/all_to_all | solution.py:238
  116.1 1.3 %unpack.1 = bf16[192,5120]{1,0:T(8,128)(2,1)} custom-call(bf16[8,192,640]{2,1,0:T(8,128)(2,1)S(1)} %all_to_all.10.refs_0_), custom_call_target="tpu_custom_call" | custom-call | bytes 3932160 | tf_op jit(solution)/shard_map/unpack/pallas_call | solution.py:225
  (2 shorter events, 0.0 us)
Async XLA Ops:
  0.6 21.0 %copy-start.3 = (s32[32,5,12]{0,2,1:T(8,128)S(1)}, s32[32,5,12]{0,2,1:T(8,128)}, u32[]{:S(2)}) copy-start(s32[32,5,12]{0,2,1:T(8,128)} %param.13) | copy-start | bytes 23044
  5.8 15.8 %collective-permute-start = (bf16[192,1152]{1,0:T(8,128)(2,1)}, bf16[192,1152]{1,0:T(8,128)(2,1)S(1)}, u32[]{:S(2)}, u32[]{:S(2)}) collective-permute-start(bf16[192,1152]{1,0:T(8,128)(2,1)} %get-tuple-element.23), channel_id=1, source_target_pairs={{0,7},{1,6},{2,1},{3,0},{4,3},{5,2},{6,5},{7,4},{8,15},{9,14},{10,... | collective-permute-start | bytes 1327112 | tf_op jit(solution)/shard_map/ppermute | solution.py:266
  9.1 19.5 %collective-permute-start.3 = (bf16[192,1152]{1,0:T(8,128)(2,1)}, bf16[192,1152]{1,0:T(8,128)(2,1)S(1)}, u32[]{:S(2)}, u32[]{:S(2)}) collective-permute-start(bf16[192,1152]{1,0:T(8,128)(2,1)} %get-tuple-element.35), channel_id=1, source_target_pairs={{0,2},{1,3},{2,4},{3,5},{4,6},{5,7},{6,0},{7,1},{8,10},{9,11},{10,... | collective-permute-start | bytes 1327112 | tf_op jit(solution)/shard_map/ppermute | solution.py:266
  10.6 23.4 %collective-permute-start.1 = (bf16[192,1152]{1,0:T(8,128)(2,1)}, bf16[192,1152]{1,0:T(8,128)(2,1)S(1)}, u32[]{:S(2)}, u32[]{:S(2)}) collective-permute-start(bf16[192,1152]{1,0:T(8,128)(2,1)} %get-tuple-element.29), channel_id=1, source_target_pairs={{0,3},{1,2},{2,5},{3,4},{4,7},{5,6},{6,1},{7,0},{8,11},{9,10},{10,... | collective-permute-start | bytes 1327112 | tf_op jit(solution)/shard_map/ppermute | solution.py:266
  11.8 50.7 %collective-permute-start.2 = (bf16[192,1152]{1,0:T(8,128)(2,1)}, bf16[192,1152]{1,0:T(8,128)(2,1)}, u32[]{:S(2)}, u32[]{:S(2)}) collective-permute-start(bf16[192,1152]{1,0:T(8,128)(2,1)} %get-tuple-element.34), channel_id=1, source_target_pairs={{0,1},{1,0},{2,3},{3,2},{4,5},{5,4},{6,7},{7,6},{8,9},{9,8},{10,11... | collective-permute-start | bytes 1327112 | tf_op jit(solution)/shard_map/ppermute | solution.py:266
  15.0 47.5 %collective-permute-start.6 = (bf16[192,1152]{1,0:T(8,128)(2,1)}, bf16[192,1152]{1,0:T(8,128)(2,1)}, u32[]{:S(2)}, u32[]{:S(2)}) collective-permute-start(bf16[192,1152]{1,0:T(8,128)(2,1)} %get-tuple-element.40), channel_id=1, source_target_pairs={{0,6},{1,7},{2,0},{3,1},{4,2},{5,3},{6,4},{7,5},{8,14},{9,15},{10,... | collective-permute-start | bytes 1327112 | tf_op jit(solution)/shard_map/ppermute | solution.py:266
  21.6 11.5 %copy-start.4 = (bf16[192,1152]{1,0:T(8,128)(2,1)}, bf16[192,1152]{1,0:T(8,128)(2,1)S(1)}, u32[]{:S(2)}) copy-start(bf16[192,1152]{1,0:T(8,128)(2,1)S(1)} %collective-permute-done.refs_7_) | copy-start | bytes 1327108
  21.8 40.8 %collective-permute-start.5 = (bf16[192,1152]{1,0:T(8,128)(2,1)}, bf16[192,1152]{1,0:T(8,128)(2,1)}, u32[]{:S(2)}, u32[]{:S(2)}) collective-permute-start(bf16[192,1152]{1,0:T(8,128)(2,1)} %get-tuple-element.39), channel_id=1, source_target_pairs={{0,5},{1,4},{2,7},{3,6},{4,1},{5,0},{6,3},{7,2},{8,13},{9,12},{10,... | collective-permute-start | bytes 1327112 | tf_op jit(solution)/shard_map/ppermute | solution.py:266
  28.6 4.5 %copy-start.5 = (bf16[192,1152]{1,0:T(8,128)(2,1)}, bf16[192,1152]{1,0:T(8,128)(2,1)S(1)}, u32[]{:S(2)}) copy-start(bf16[192,1152]{1,0:T(8,128)(2,1)S(1)} %collective-permute-done.3.refs_2_) | copy-start | bytes 1327108
  28.6 34.0 %collective-permute-start.4 = (bf16[192,1152]{1,0:T(8,128)(2,1)}, bf16[192,1152]{1,0:T(8,128)(2,1)}, u32[]{:S(2)}, u32[]{:S(2)}) collective-permute-start(bf16[192,1152]{1,0:T(8,128)(2,1)} %get-tuple-element.37), channel_id=1, source_target_pairs={{0,4},{1,5},{2,6},{3,7},{4,0},{5,1},{6,2},{7,3},{8,12},{9,13},{10,... | collective-permute-start | bytes 1327112 | tf_op jit(solution)/shard_map/ppermute | solution.py:266
  33.1 24.4 %copy-start.2 = (s32[32,5,12,12]{0,3,2,1:T(8,128)S(1)}, s32[32,5,12,12]{0,3,2,1:T(8,128)}, u32[]{:S(2)}) copy-start(s32[32,5,12,12]{0,3,2,1:T(8,128)} %param.12) | copy-start | bytes 276484
  34.0 0.8 copy-start.6
  34.8 44.6 %all-to-all-start = ((bf16[8,192,768]{2,1,0:T(8,128)(2,1)}), bf16[8,192,768]{2,1,0:T(8,128)(2,1)S(1)}, u32[]{:S(2)}, u32[]{:S(2)}) async-start(bf16[8,192,768]{2,1,0:T(8,128)(2,1)} %pack_3.1), calls=%async_computation | async-start | bytes 4718592 | tf_op jit(solution)/shard_map/all_to_all | solution.py:238
  62.6 16.9 %copy-start.1 = (f32[5,12,1536]{2,1,0:T(8,128)S(1)}, f32[5,12,1536]{2,1,0:T(8,128)}, u32[]{:S(2)}) copy-start(f32[5,12,1536]{2,1,0:T(8,128)} %broadcast_select_fusion.bias_ref) | copy-start | bytes 1105924
  79.4 1.5 %copy-start = (bf16[1536,640]{1,0:T(8,128)(2,1)S(1)}, bf16[1536,640]{1,0:T(8,128)(2,1)}, u32[]{:S(2)}) copy-start(bf16[1536,640]{1,0:T(8,128)(2,1)} %attend_3.1.mixed_ref) | copy-start | bytes 5898244
